TPU v7x, 32 devices: a whole 2x2x4 slice. The times are simulated.
32 devices in a mesh: dp: 16 (over z, y, core), fsdp: 2 (over x).
Axes of the slice: x: 2, y: 2, z: 4, core: 2. Of those that a mesh axis runs over, the one named last changes fastest.
Arguments:
- block_input: bfloat16 [512, 784, 192], P(('dp', 'fsdp')), may hold values from -6 to 6
- token_crop: int32 [512, 784], P(('dp', 'fsdp')), may hold values from 0 to 3, as said below
- key_crop: int32 [512, 196], P(('dp', 'fsdp')), may hold values from 0 to 3, as said below
- first_gain: float32 [192], replicated, may hold values from 0.25 to 1.75
- first_bias: float32 [192], replicated, may hold values from -1.75 to 1.75
- qkv_weight: bfloat16 [192, 576], P('fsdp', 'dp'), may hold values from -0.4375 to 0.4375
- qkv_bias: float32 [576], replicated, may hold values from -1.75 to 1.75
- pool_kernel: float32 [2, 9, 96], replicated, may hold values from -2 to 2
- pool_gain: float32 [2, 96], replicated, may hold values from 0.25 to 1.75
- pool_bias: float32 [2, 96], replicated, may hold values from -1.75 to 1.75
- rel_height: float32 [55, 96], replicated, may hold values from -0.625 to 0.625
- rel_width: float32 [55, 96], replicated, may hold values from -0.625 to 0.625
- proj_weight: bfloat16 [192, 192], P('fsdp', 'dp'), may hold values from -0.4375 to 0.4375
- proj_bias: float32 [192], replicated, may hold values from -1.75 to 1.75
- second_gain: float32 [192], replicated, may hold values from 0.25 to 1.75
- second_bias: float32 [192], replicated, may hold values from -1.75 to 1.75
- fc1_weight: bfloat16 [192, 768], P('fsdp', 'dp'), may hold values from -0.4375 to 0.4375
- fc1_bias: float32 [768], replicated, may hold values from -3 to 3
- fc2_weight: bfloat16 [768, 192], P('fsdp', 'dp'), may hold values from -0.21875 to 0.21875
- fc2_bias: float32 [192], replicated, may hold values from -1.75 to 1.75
- cotangent: bfloat16 [512, 784, 192], P(('dp', 'fsdp')), may hold values from -18 to 18
Outputs:
- block_output: bfloat16 [512, 784, 192], P(('dp', 'fsdp'))
- input_grad: float32 [512, 784, 192], P(('dp', 'fsdp'))
- grad_first_gain: float32 [192], replicated
- grad_first_bias: float32 [192], replicated
- grad_qkv_weight: float32 [192, 576], P('fsdp', 'dp')
- grad_qkv_bias: float32 [576], replicated
- grad_pool_kernel: float32 [2, 9, 96], replicated
- grad_pool_gain: float32 [2, 96], replicated
- grad_pool_bias: float32 [2, 96], replicated
- grad_rel_height: float32 [55, 96], replicated
- grad_rel_width: float32 [55, 96], replicated
- grad_proj_weight: float32 [192, 192], P('fsdp', 'dp')
- grad_proj_bias: float32 [192], replicated
- grad_second_gain: float32 [192], replicated
- grad_second_bias: float32 [192], replicated
- grad_fc1_weight: float32 [192, 768], P('fsdp', 'dp')
- grad_fc1_bias: float32 [768], replicated
- grad_fc2_weight: float32 [768, 192], P('fsdp', 'dp')
- grad_fc2_bias: float32 [192], replicated
Inputs may be any that keep to these rules, and one draw needn't show every extreme that they name: `token_crop`: each canvas is cut into four rectangular crops by one row cut and one column cut, each at an even position from 2 to 26; a token's crop id is 2 (row at or below the row cut) + (column at or right of the column cut). `key_crop`: pooled key (i, j) of a canvas carries the crop id of token (2 i, 2 j) of that canvas.
All inputs are finite; a program needn't handle non-finite values.
Results may differ from a plain program's by a relative error of at most 0.017.
Values may be sent and summed in bfloat16 or wider, within the bound.
A program may use at most 384 MiB of HBM per device.

v0:
```python
import jax
import jax.numpy as jnp
from jax import lax
from jax.sharding import PartitionSpec as P

D = 192
HEADS = 2
HD = 96
SIDE = 28
KS = 14
NTOK = 784
NKEY = 196


layer_eps = 1e-06
masked_fill = -1e30
highest = lax.Precision.HIGHEST


def layer_norm(values, norm_gain, norm_shift):
    center = values - jnp.mean(values, -1, keepdims=True)
    spread = jnp.mean(center * center, -1, keepdims=True)
    return center * lax.rsqrt(spread + layer_eps) * norm_gain + norm_shift


def lane_blocks(width):
    group = jnp.arange(width, dtype=jnp.int32) // HD
    return (group[:, None] == group[None, :]).astype(jnp.float32) / HD


def shift_down(values, axis):
    size = values.shape[axis]
    kept = lax.slice_in_dim(values, 0, size - 1, 1, axis)
    zero_shape = list(values.shape)
    zero_shape[axis] = 1
    return jnp.concatenate((jnp.zeros(tuple(zero_shape), values.dtype), kept), axis)


def pool_pair(kv_raw, pool_kernel, pool_gain, pool_bias):
    canvases = kv_raw.shape[0]
    width = kv_raw.shape[-1]
    lanes = jnp.broadcast_to(pool_kernel[:, :, None, :], (2, 9, HEADS, HD))
    lanes = jnp.transpose(lanes, (1, 0, 2, 3)).reshape(9, width)
    gains = jnp.broadcast_to(pool_gain[:, None, :], (2, HEADS, HD)).reshape(width)
    shifts = jnp.broadcast_to(pool_bias[:, None, :], (2, HEADS, HD)).reshape(width)
    grid = kv_raw.reshape(canvases, KS, 2, KS, 2, width)

    def tap(row_tap, col_tap):
        row_parity = 0 if row_tap == 1 else 1
        col_parity = 0 if col_tap == 1 else 1
        picked = grid[:, :, row_parity][:, :, :, col_parity]
        return picked * lanes[3 * row_tap + col_tap]

    inner = tap(1, 1) + tap(1, 2) + tap(2, 1) + tap(2, 2)
    row_edge = tap(0, 1) + tap(0, 2) + shift_down(tap(0, 0), 2)
    col_edge = tap(1, 0) + tap(2, 0)
    pooled = inner + shift_down(col_edge, 2) + shift_down(row_edge, 1)
    blocks = lane_blocks(width)
    center = pooled - jnp.dot(pooled, blocks, precision=highest)
    spread = jnp.dot(center * center, blocks, precision=highest)
    return center * lax.rsqrt(spread + layer_eps) * gains + shifts


def gelu_exact(values):
    return jax.nn.gelu(values, approximate=False)


def table_rows(rel_table):
    table_index = (
        jnp.arange(SIDE, dtype=jnp.int32)[:, None]
        - 2 * jnp.arange(KS, dtype=jnp.int32)[None, :]
        + 2 * (KS - 1)
    )
    onehot = (
        table_index[:, :, None] == jnp.arange(rel_table.shape[0], dtype=jnp.int32)[None, None, :]
    )
    return jnp.einsum("xkr,rd->xkd", onehot.astype(jnp.float32), rel_table, precision=highest)


def both_tables(rel_height, rel_width):
    return (table_rows(rel_height), table_rows(rel_width))


def canvas_scores(queries, keys_pooled, rows_h, rows_w, token_ids, key_ids):
    content = jnp.einsum(
        "qhd,khd->hqk", queries, keys_pooled, preferred_element_type=jnp.float32
    ) * HD ** (-0.5)
    grid_q = queries.astype(jnp.float32).reshape(SIDE, SIDE, HEADS, HD)
    along_h = jnp.einsum("xyhd,xkd->hxyk", grid_q, rows_h, precision=highest)
    along_w = jnp.einsum("xyhd,ykd->hxyk", grid_q, rows_w, precision=highest)
    scores = (
        content.reshape(HEADS, SIDE, SIDE, KS, KS) + along_h[..., :, None] + along_w[..., None, :]
    )
    scores = scores.reshape(HEADS, NTOK, NKEY)
    same_crop = token_ids[:, None] == key_ids[None, :]
    return (jnp.where(same_crop[None], scores, masked_fill), grid_q)


def fetch_attention(qkv_weight, proj_weight):
    columns = (
        lax.all_gather(qkv_weight, "dp", axis=1, tiled=True),
        lax.all_gather(proj_weight, "dp", axis=1, tiled=True),
    )
    return (
        lax.all_gather(columns[0], "fsdp", axis=0, tiled=True),
        lax.all_gather(columns[1], "fsdp", axis=0, tiled=True),
    )


def fetch_mlp(fc1_weight, fc2_weight):
    columns = (
        lax.all_gather(fc1_weight, "dp", axis=1, tiled=True),
        lax.all_gather(fc2_weight, "dp", axis=1, tiled=True),
    )
    return (
        lax.all_gather(columns[0], "fsdp", axis=0, tiled=True),
        lax.all_gather(columns[1], "fsdp", axis=0, tiled=True),
    )


def local(
    block_input,
    token_crop,
    key_crop,
    first_gain,
    first_bias,
    qkv_weight,
    qkv_bias,
    pool_kernel,
    pool_gain,
    pool_bias,
    rel_height,
    rel_width,
    proj_weight,
    proj_bias,
    second_gain,
    second_bias,
    fc1_weight,
    fc1_bias,
    fc2_weight,
    fc2_bias,
    cotangent,
):
    canvases = block_input.shape[0]
    row_count = canvases * NTOK
    score_scale = HD ** (-0.5)
    qkv_full, proj_full = fetch_attention(qkv_weight, proj_weight)
    token_rows = block_input.reshape(row_count, D).astype(jnp.float32)
    normed, first_back = jax.vjp(layer_norm, token_rows, first_gain, first_bias)
    normed = normed.astype(jnp.bfloat16)
    packed = jnp.dot(normed, qkv_full, preferred_element_type=jnp.float32) + qkv_bias
    queries = packed[:, :D].astype(jnp.bfloat16).reshape(canvases, NTOK, HEADS, HD)
    kv_raw = packed[:, D:].reshape(canvases, SIDE, SIDE, 2 * D)
    pooled, pool_back = jax.vjp(pool_pair, kv_raw, pool_kernel, pool_gain, pool_bias)
    pooled = pooled.astype(jnp.bfloat16)
    keys_pooled = pooled[..., :D].reshape(canvases, NKEY, HEADS, HD)
    values_pooled = pooled[..., D:].reshape(canvases, NKEY, HEADS, HD)
    table_pair, table_back = jax.vjp(both_tables, rel_height, rel_width)
    rows_h, rows_w = table_pair

    def attend(canvas_item):
        queries_one, keys_one, values_one, token_ids, key_ids = canvas_item
        scores, grid_q = canvas_scores(queries_one, keys_one, rows_h, rows_w, token_ids, key_ids)
        row_max = jnp.max(scores, -1, keepdims=True)
        exponent = jnp.exp(scores - row_max)
        row_total = jnp.sum(exponent, -1, keepdims=True)
        probs = (exponent / row_total).astype(jnp.bfloat16)
        mixed_heads = jnp.einsum(
            "hqk,khd->qhd", probs, values_one, preferred_element_type=jnp.float32
        )
        mixed_heads = mixed_heads + grid_q.reshape(NTOK, HEADS, HD)
        return (mixed_heads.astype(jnp.bfloat16), (row_max + jnp.log(row_total))[..., 0])

    mixed_heads, logsum = lax.map(
        attend, (queries, keys_pooled, values_pooled, token_crop, key_crop)
    )
    attended = mixed_heads.reshape(row_count, D)
    middle = (
        token_rows + jnp.dot(attended, proj_full, preferred_element_type=jnp.float32) + proj_bias
    )
    fc1_full, fc2_full = fetch_mlp(fc1_weight, fc2_weight)
    normed_second, second_back = jax.vjp(layer_norm, middle, second_gain, second_bias)
    normed_second = normed_second.astype(jnp.bfloat16)
    hidden = jnp.dot(normed_second, fc1_full, preferred_element_type=jnp.float32) + fc1_bias
    activated, gelu_back = jax.vjp(gelu_exact, hidden)
    activated = activated.astype(jnp.bfloat16)
    output = middle + jnp.dot(activated, fc2_full, preferred_element_type=jnp.float32) + fc2_bias
    block_output = output.astype(jnp.bfloat16).reshape(canvases, NTOK, D)
    fc1_full, fc2_full = fetch_mlp(fc1_weight, fc2_weight)
    grad_out = cotangent.reshape(row_count, D)
    grad_fc2_weight = jnp.einsum(
        "tf,td->fd", activated, grad_out, preferred_element_type=jnp.float32
    )
    grad_fc2_bias = jnp.sum(grad_out.astype(jnp.float32), 0)
    grad_activated = jnp.einsum("td,fd->tf", grad_out, fc2_full, preferred_element_type=jnp.float32)
    grad_hidden = gelu_back(grad_activated)[0].astype(jnp.bfloat16)
    grad_fc1_weight = jnp.einsum(
        "te,tf->ef", normed_second, grad_hidden, preferred_element_type=jnp.float32
    )
    grad_fc1_bias = jnp.sum(grad_hidden.astype(jnp.float32), 0)
    grad_normed_second = jnp.einsum(
        "tf,ef->te", grad_hidden, fc1_full, preferred_element_type=jnp.float32
    )
    grad_middle_norm, grad_second_gain, grad_second_bias = second_back(grad_normed_second)
    grad_middle = grad_out.astype(jnp.float32) + grad_middle_norm
    grad_branch = grad_middle.astype(jnp.bfloat16)
    grad_proj_weight = jnp.einsum(
        "te,tf->ef", attended, grad_branch, preferred_element_type=jnp.float32
    )
    grad_proj_bias = jnp.sum(grad_branch.astype(jnp.float32), 0)
    qkv_full, proj_full = fetch_attention(qkv_weight, proj_weight)
    grad_attended = jnp.einsum(
        "tf,ef->te", grad_branch, proj_full, preferred_element_type=jnp.float32
    )
    grad_attended = grad_attended.astype(jnp.bfloat16).reshape(canvases, NTOK, HEADS, HD)

    def attend_back(table_grads, canvas_item):
        queries_one, keys_one, values_one, token_ids, key_ids, logsum_one, grad_one = canvas_item
        scores, grid_q = canvas_scores(queries_one, keys_one, rows_h, rows_w, token_ids, key_ids)
        probs = jnp.exp(scores - logsum_one[..., None])
        grad_probs = jnp.einsum(
            "qhd,khd->hqk", grad_one, values_one, preferred_element_type=jnp.float32
        )
        grad_values = jnp.einsum(
            "hqk,qhd->khd", probs.astype(jnp.bfloat16), grad_one, preferred_element_type=jnp.float32
        )
        inner_sum = jnp.sum(probs * grad_probs, -1, keepdims=True)
        grad_scores = (probs * (grad_probs - inner_sum)).astype(jnp.bfloat16)
        grad_keys = (
            jnp.einsum("hqk,qhd->khd", grad_scores, queries_one, preferred_element_type=jnp.float32)
            * score_scale
        )
        grid_grads = grad_scores.astype(jnp.float32).reshape(HEADS, SIDE, SIDE, KS, KS)
        sum_h = jnp.sum(grid_grads, -1)
        sum_w = jnp.sum(grid_grads, -2)
        from_tables = jnp.einsum("hxyk,xkd->xyhd", sum_h, rows_h, precision=highest) + jnp.einsum(
            "hxyk,ykd->xyhd", sum_w, rows_w, precision=highest
        )
        grad_queries = (
            jnp.einsum("hqk,khd->qhd", grad_scores, keys_one, preferred_element_type=jnp.float32)
            * score_scale
            + grad_one.astype(jnp.float32)
            + from_tables.reshape(NTOK, HEADS, HD)
        )
        table_grads = (
            table_grads[0] + jnp.einsum("hxyk,xyhd->xkd", sum_h, grid_q, precision=highest),
            table_grads[1] + jnp.einsum("hxyk,xyhd->ykd", sum_w, grid_q, precision=highest),
        )
        return (table_grads, (grad_queries, grad_keys, grad_values))

    zeros_table = jnp.zeros((SIDE, KS, HD), jnp.float32)
    table_grads, per_canvas = lax.scan(
        attend_back,
        (zeros_table, zeros_table),
        (queries, keys_pooled, values_pooled, token_crop, key_crop, logsum, grad_attended),
    )
    grad_queries, grad_keys, grad_values = per_canvas
    grad_rel_height, grad_rel_width = table_back(table_grads)
    grad_pooled = jnp.concatenate(
        (grad_keys.reshape(canvases, KS, KS, D), grad_values.reshape(canvases, KS, KS, D)), -1
    )
    grad_kv_raw, grad_pool_kernel, grad_pool_gain, grad_pool_bias = pool_back(grad_pooled)
    grad_packed = jnp.concatenate(
        (grad_queries.reshape(row_count, D), grad_kv_raw.reshape(row_count, 2 * D)), -1
    )
    grad_packed = grad_packed.astype(jnp.bfloat16)
    grad_qkv_weight = jnp.einsum(
        "te,tf->ef", normed, grad_packed, preferred_element_type=jnp.float32
    )
    grad_qkv_bias = jnp.sum(grad_packed.astype(jnp.float32), 0)
    grad_normed = jnp.einsum("tf,ef->te", grad_packed, qkv_full, preferred_element_type=jnp.float32)
    grad_rows_norm, grad_first_gain, grad_first_bias = first_back(grad_normed)
    input_grad = (grad_middle + grad_rows_norm).reshape(canvases, NTOK, D)
    partial_sums = (
        lax.psum_scatter(
            grad_qkv_weight.astype(jnp.bfloat16), "fsdp", scatter_dimension=0, tiled=True
        ).astype(jnp.float32),
        lax.psum_scatter(
            grad_proj_weight.astype(jnp.bfloat16), "fsdp", scatter_dimension=0, tiled=True
        ).astype(jnp.float32),
        lax.psum_scatter(
            grad_fc1_weight.astype(jnp.bfloat16), "fsdp", scatter_dimension=0, tiled=True
        ).astype(jnp.float32),
        lax.psum_scatter(
            grad_fc2_weight.astype(jnp.bfloat16), "fsdp", scatter_dimension=0, tiled=True
        ).astype(jnp.float32),
    )
    owned = (
        lax.psum_scatter(
            partial_sums[0].astype(jnp.bfloat16), "dp", scatter_dimension=1, tiled=True
        ).astype(jnp.float32),
        lax.psum_scatter(
            partial_sums[1].astype(jnp.bfloat16), "dp", scatter_dimension=1, tiled=True
        ).astype(jnp.float32),
        lax.psum_scatter(
            partial_sums[2].astype(jnp.bfloat16), "dp", scatter_dimension=1, tiled=True
        ).astype(jnp.float32),
        lax.psum_scatter(
            partial_sums[3].astype(jnp.bfloat16), "dp", scatter_dimension=1, tiled=True
        ).astype(jnp.float32),
    )
    summed_small = lax.psum(
        (
            grad_first_gain,
            grad_first_bias,
            grad_qkv_bias,
            grad_pool_kernel,
            grad_pool_gain,
            grad_pool_bias,
            grad_rel_height,
            grad_rel_width,
            grad_proj_bias,
            grad_second_gain,
            grad_second_bias,
            grad_fc1_bias,
            grad_fc2_bias,
        ),
        ("dp", "fsdp"),
    )
    return (
        block_output,
        input_grad,
        summed_small[0],
        summed_small[1],
        owned[0],
        summed_small[2],
        summed_small[3],
        summed_small[4],
        summed_small[5],
        summed_small[6],
        summed_small[7],
        owned[1],
        summed_small[8],
        summed_small[9],
        summed_small[10],
        owned[2],
        summed_small[11],
        owned[3],
        summed_small[12],
    )


def solution(mesh):
    return jax.shard_map(
        local,
        mesh=mesh,
        in_specs=(
            P(("dp", "fsdp"), None, None),
            P(("dp", "fsdp"), None),
            P(("dp", "fsdp"), None),
            P(),
            P(),
            P("fsdp", "dp"),
            P(),
            P(),
            P(),
            P(),
            P(),
            P(),
            P("fsdp", "dp"),
            P(),
            P(),
            P(),
            P("fsdp", "dp"),
            P(),
            P("fsdp", "dp"),
            P(),
            P(("dp", "fsdp"), None, None),
        ),
        out_specs=(
            P(("dp", "fsdp"), None, None),
            P(("dp", "fsdp"), None, None),
            P(),
            P(),
            P("fsdp", "dp"),
            P(),
            P(),
            P(),
            P(),
            P(),
            P(),
            P("fsdp", "dp"),
            P(),
            P(),
            P(),
            P("fsdp", "dp"),
            P(),
            P("fsdp", "dp"),
            P(),
        ),
        check_vma=False,
    )
```

profile of v0, /device:TPU:0, one launch (start us, length us, event | category | flops | bytes accessed | tf_op | source)
XLA Modules:
  0.0 2980.8 jit_solution(6609934568488212422)
XLA Ops:
  32.8 23.5 all-gather
  62.8 17.6 convolution_add_fusion
  80.4 14.7 slice.110
  101.6 19.5 copy.244
  121.1 22.4 reshape_reshape.3
  143.6 15.0 fusion.169
  196.6 15.0 convolution_subtract_fusion
  211.6 13.8 add_convert_fusion.4
  262.9 575.2 %while.31 = (s32[]{:T(128)}, bf16[16,784,2,96]{1,3,2,0:T(8,128)(2,1)}, f32[16,2,784]{2,1,0:T(2,128)}, bf16[16,196,2,96]{1,3,2,0:T(8,128)(2,1)}, s32[16,784]{1,0:...) while((s32[]{:T(128)}, ...), condition=%wide.region_5.6_spmd, body=%wide.region_2.5_spmd.sunk | while | flops 172268320 | bytes 17958952 | solution.py:174
  855.8 17.3 all-gather.1
  890.0 19.6 all_gather.36
  934.2 17.6 all-gather.2
  958.8 91.6 %multiply_convert_fusion.1 = (bf16[12544,768]{1,0:T(8,128)(2,1)}, f32[12544,768]{1,0:T(8,128)}, f32[12544,768]{1,0:T(8,128)}) fusion(f32[768]{0:T(1024)S(1)} %copy-done.82, bf16[192,768]{1,0:T(8,128)(2,1)S(1)} %all_gather.37, f32[12544,192]{0,1:T(8,128)} %copy-done.3, f32[192]{0:T(256)S(1)} %copy-done.83, f32[192]{0:T(256)S(1)} %copy-done.76, ...), kind=kOutput, calls=%fused_computation.97 | convolution fusion | flops 4347248640 | bytes 106371584 | tf_op jit(solution)/shard_map/dot_general | solution.py:184
  1050.4 37.7 %convert_reduce_fusion = (f32[768]{0:T(1024)}, bf16[12544,768]{1,0:T(8,128)(2,1)}) fusion(f32[12544,768]{1,0:T(8,128)} %get-tuple-element.523, bf16[12544,192]{0,1:T(8,128)(2,1)} %reshape.433, bf16[768,192]{0,1:T(8,128)(2,1)S(1)} %copy-done.16, f32[12544,768]{1,0:T(8,128)} %get-tuple-element.560, f32[768]{0:T(1024)S(1)} %copy-done.82), kind=kOutput, calls=%fused_computation.95 | convolution fusion | flops 3863149824 | bytes 101455872 | tf_op jit(solution)/shard_map/td,fd->tf/dot_general | solution.py:195
  1088.0 15.6 multiply_reduce_fusion.2
  1154.3 1175.1 %while.32 = (s32[]{:T(128)}, f32[28,14,96]{2,1,0:T(8,128)}, f32[28,14,96]{2,1,0:T(8,128)}, bf16[16,784,2,96]{1,3,2,0:T(8,128)(2,1)}, f32[16,196,2,96]{1,3,2,0:T(...) while((s32[]{:T(128)}, f32[28,14,96]{2,1,0:T(8,128)}, ...), condition=%wide.region_14.15_spmd.clone, body=%wide.region_10.14_spmd.clone.sunk | while | flops 451811360 | bytes 39596472 | solution.py:252
  2350.8 17.9 add_add_fusion.4
  2392.5 22.1 multiply_reduce_fusion.13
  2461.5 26.6 add_convert_fusion.1
  2488.1 18.7 copy.266
  2506.8 20.2 reshape.438
  2527.1 18.3 copy.285
  2558.6 13.8 fusion.105
  2585.6 14.3 convolution_convert_fusion.2
  2617.5 15.5 fusion.164
  2644.3 13.6 add_add_fusion.2
  2684.2 21.3 fusion.75
  2727.2 40.7 %all-reduce.37 = (f32[192]{0:T(256)}, f32[192]{0:T(256)}, f32[576]{0:T(1024)}, f32[2,9,96]{2,0,1:T(2,128)}, f32[2,96]{1,0:T(2,128)}, /*index=5*/f32[2,96]{1,0:T(...) all-reduce(f32[192]{0:T(256)S(1)} %get-tuple-element.430, ...), channel_id=1, replica_groups=mesh['dp'=16,'fsdp'=2] {'dp','fsdp'}, use_global_device_ids=true, to_apply=%region_18.19 | all-reduce | flops 15168 | bytes 121344 | tf_op jit(solution)/shard_map/psum | solution.py:302
  2767.9 59.9 %all-reduce.34 = bf16[96,192]{1,0:T(8,128)(2,1)S(1)} all-reduce(bf16[96,192]{1,0:T(8,128)(2,1)} %reduce-scatter.16.cloned.1.call-done), channel_id=5, replica_groups=mesh['dp'=16,'fsdp'=2] {'dp'}, use_global_device_ids=true, to_apply=%region_45.46.clone | all-reduce | flops 18432 | bytes 73728
  2829.7 30.6 %fusion = bf16[384,16]{0,1:T(8,128)(2,1)S(1)} fusion(bf16[384,192]{0,1:T(8,128)(2,1)S(1)} %copy.293), kind=kCustom, calls=%all-reduce-scatter | all-reduce-scatter fusion | flops 98305 | bytes 160256
  2867.5 44.8 %all-reduce.40.cloned.1.call-done = bf16[96,576]{1,0:T(8,128)(2,1)} async-done(((bf16[96,576]{1,0:T(8,128)(2,1)}), bf16[96,576]{1,0:T(8,128)(2,1)}) %all-reduce.40.cloned.1.call-update) | async-done | bytes 110608
  2915.2 56.7 %reduce-scatter.20.cloned.1.call-done = bf16[48,96]{1,0:T(8,128)(2,1)} async-done(((bf16[768,96]{1,0:T(8,128)(2,1)}), bf16[48,96]{1,0:T(8,128)(2,1)}) %reduce-scatter.20.cloned.1.call-update) | async-done | bytes 9232
  (1211 shorter events, 2184.8 us)
Async XLA Ops:
  7.2 254.5 %copy-start = (f32[55,96]{1,0:T(8,128)S(1)}, f32[55,96]{1,0:T(8,128)}, u32[]{:S(2)}) copy-start(f32[55,96]{1,0:T(8,128)} %param.36) | copy-start | bytes 63364
  7.2 2760.7 %reduce-scatter.16.cloned.1.call-start = ((), (), s32[]{:S(2)}) async-start(), calls=%async_computation.6 | async-start | bytes 147456 | tf_op jit(solution)/shard_map/reduce_scatter | solution.py:278
  20.0 42.8 %copy-start.22 = (f32[12544]{0:T(1024)}, f32[12544]{0:T(1024)S(1)}, u32[]{:S(2)}) copy-start(f32[12544]{0:T(1024)S(1)} %div.82) | copy-start | bytes 150532
  20.0 191.6 %copy-start.38 = (s32[384]{0:T(512)}, s32[384]{0:T(512)S(1)}, u32[]{:S(2)}) copy-start(s32[384]{0:T(512)S(1)} %add_select_fusion) | copy-start | bytes 4612
  20.0 42.7 %copy-start.59 = (f32[576]{0:T(1024)S(1)}, f32[576]{0:T(1024)}, u32[]{:S(2)}) copy-start(f32[576]{0:T(1024)} %param.31) | copy-start | bytes 6916
  20.0 42.7 %copy-start.60 = (f32[192]{0:T(256)S(1)}, f32[192]{0:T(256)}, u32[]{:S(2)}) copy-start(f32[192]{0:T(256)} %param.28) | copy-start | bytes 2308
  20.1 42.7 %copy-start.70 = (f32[192]{0:T(256)S(1)}, f32[192]{0:T(256)}, u32[]{:S(2)}) copy-start(f32[192]{0:T(256)} %param.29) | copy-start | bytes 2308
  32.8 47.6 %copy-start.24 = (f32[12544]{0:T(1024)}, f32[12544]{0:T(1024)S(1)}, u32[]{:S(2)}) copy-start(f32[12544]{0:T(1024)S(1)} %rsqrt.23) | copy-start | bytes 150532
  178.9 32.7 %copy-start.67 = (f32[384]{0:T(512)}, f32[384]{0:T(512)S(1)}, u32[]{:S(2)}) copy-start(f32[384]{0:T(512)S(1)} %mul.425) | copy-start | bytes 4612
  237.4 25.2 copy-start.40
  838.1 39.8 %copy-start.69 = (f32[192]{0:T(256)S(1)}, f32[192]{0:T(256)}, u32[]{:S(2)}) copy-start(f32[192]{0:T(256)} %param.38) | copy-start | bytes 2308
  884.8 218.9 %copy-start.32 = (f32[12544]{0:T(1024)}, f32[12544]{0:T(1024)S(1)}, u32[]{:S(2)}) copy-start(f32[12544]{0:T(1024)S(1)} %broadcast_multiply_fusion.1) | copy-start | bytes 150532
  890.0 213.7 %copy-start.34 = (f32[12544]{0:T(1024)}, f32[12544]{0:T(1024)S(1)}, u32[]{:S(2)}) copy-start(f32[12544]{0:T(1024)S(1)} %fusion.142) | copy-start | bytes 150532
  916.5 42.2 %copy-start.76 = (f32[192]{0:T(256)S(1)}, f32[192]{0:T(256)}, u32[]{:S(2)}) copy-start(f32[192]{0:T(256)} %param.39) | copy-start | bytes 2308
  916.5 42.2 %copy-start.82 = (f32[768]{0:T(1024)S(1)}, f32[768]{0:T(1024)}, u32[]{:S(2)}) copy-start(f32[768]{0:T(1024)} %param.42) | copy-start | bytes 9220
  916.5 42.2 %copy-start.83 = (f32[192]{0:T(256)S(1)}, f32[192]{0:T(256)}, u32[]{:S(2)}) copy-start(f32[192]{0:T(256)} %param.40) | copy-start | bytes 2308
  958.7 91.6 %copy-start.16 = (bf16[768,192]{0,1:T(8,128)(2,1)S(1)}, bf16[768,192]{0,1:T(8,128)(2,1)}, u32[]{:S(2)}) copy-start(bf16[768,192]{0,1:T(8,128)(2,1)} %all_gather.39) | copy-start | bytes 884740
  1131.5 1697.0 %reduce-scatter.14.cloned.1.call-start = ((), (), s32[]{:S(2)}) async-start(), calls=%async_computation.5 | async-start | bytes 368640 | tf_op jit(solution)/shard_map/reduce_scatter | solution.py:275
  2339.3 29.5 copy-start.11
  2527.1 31.6 %copy-start.23 = (f32[12544]{0:T(1024)S(1)}, f32[12544]{0:T(1024)}, u32[]{:S(2)}) copy-start(f32[12544]{0:T(1024)} %copy-done.22) | copy-start | bytes 150532
  2527.1 31.6 %copy-start.25 = (f32[12544]{0:T(1024)S(1)}, f32[12544]{0:T(1024)}, u32[]{:S(2)}) copy-start(f32[12544]{0:T(1024)} %copy-done.24) | copy-start | bytes 150532
  2527.1 31.6 %copy-start.61 = (f32[192]{0:T(256)S(1)}, f32[192]{0:T(256)}, u32[]{:S(2)}) copy-start(f32[192]{0:T(256)} %param.28) | copy-start | bytes 2308
  2527.1 31.6 %copy-start.71 = (f32[192]{0:T(256)S(1)}, f32[192]{0:T(256)}, u32[]{:S(2)}) copy-start(f32[192]{0:T(256)} %param.29) | copy-start | bytes 2308
  2572.5 256.1 %reduce-scatter.22.cloned.1.call-start = ((), (), s32[]{:S(2)}) async-start(), calls=%async_computation.9 | async-start | bytes 589824
  2585.5 280.3 %reduce-scatter.18.cloned.1.call-start = ((), (), s32[]{:S(2)}) async-start(), calls=%async_computation.7 | async-start | bytes 442368 | tf_op jit(solution)/shard_map/reduce_scatter | solution.py:281
  2599.9 312.4 %all-reduce.40.cloned.1.call-start = ((), (), s32[]{:S(2)}) async-start(), calls=%async_computation.10 | async-start | bytes 245760
  2705.5 268.0 %copy-start.1 = (f32[55,96]{1,0:T(8,128)S(1)}, f32[55,96]{1,0:T(8,128)}, u32[]{:S(2)}) copy-start(f32[55,96]{1,0:T(8,128)} %param.36) | copy-start | bytes 63364
  2828.5 143.4 %reduce-scatter.20.cloned.1.call-start = ((), (), s32[]{:S(2)}) async-start(), calls=%async_computation.8 | async-start | bytes 208896
  2860.3 53.7 %collective-permute-start = (bf16[384,16]{0,1:T(8,128)(2,1)S(1)}, bf16[384,16]{0,1:T(8,128)(2,1)S(1)}, u32[]{:S(2)}, u32[]{:S(2)}) collective-permute-start(bf16[384,16]{0,1:T(8,128)(2,1)S(1)} %fusion), channel_id=1, source_target_pairs={{0,2},{2,4},{4,6},{6,8},{8,10},{10,12},{12,14},{14,16},{16,18},{18... | collective-permute-start | bytes 36872
  2861.8 52.1 %collective-permute-start.1 = (bf16[384,16]{0,1:T(8,128)(2,1)S(1)}, bf16[384,16]{0,1:T(8,128)(2,1)S(1)}, u32[]{:S(2)}, u32[]{:S(2)}) collective-permute-start(bf16[384,16]{0,1:T(8,128)(2,1)S(1)} %fusion), channel_id=1, source_target_pairs={{0,4},{2,6},{4,8},{6,10},{8,12},{10,14},{12,16},{14,18},{16,20},{1... | collective-permute-start | bytes 36872
  2863.1 50.8 %collective-permute-start.2 = (bf16[384,16]{0,1:T(8,128)(2,1)S(1)}, bf16[384,16]{0,1:T(8,128)(2,1)S(1)}, u32[]{:S(2)}, u32[]{:S(2)}) collective-permute-start(bf16[384,16]{0,1:T(8,128)(2,1)S(1)} %fusion), channel_id=1, source_target_pairs={{0,6},{2,8},{4,10},{6,12},{8,14},{10,16},{12,18},{14,20},{16,22},{... | collective-permute-start | bytes 36872
  2864.4 49.5 %collective-permute-start.3 = (bf16[384,12]{0,1:T(8,128)(2,1)S(1)}, bf16[384,12]{0,1:T(8,128)(2,1)S(1)}, u32[]{:S(2)}, u32[]{:S(2)}) collective-permute-start(bf16[384,12]{0,1:T(8,128)(2,1)S(1)} %slice.134), channel_id=1, source_target_pairs={{0,8},{2,10},{4,12},{6,14},{8,16},{10,18},{12,20},{14,22},{16,24},... | collective-permute-start | bytes 27656
  (130 other events, 1602.6 us)
Sparse Core Ops, SparseCore 0:
  1131.6 8.6 reduce-scatter.15
  2572.6 10.2 reduce-scatter.13
  2585.6 12.5 reduce-scatter.21
  2600.4 12.0 reduce-scatter.17
  2828.7 83.6 all-reduce.39
  2916.1 55.8 reduce-scatter.19
where the time goes:
time: 3010 us; the launch traced here: 2980 us
  local copies, waits for them, and re-layouts  1520 us (50%)
  matrix products  825 us (27%)
  other arithmetic  274 us (9%)
  blocking collectives  234 us (8%)
  waiting for transfers between devices  102 us (3%)
    add x128, local copies, waits for them, and re-layouts, canvas_scores(): content.reshape(HEADS, SIDE, SIDE, KS, KS) + along_h[..., :, None]  696 us
    reshape x16, local copies, waits for them, and re-layouts, attend_back(): grad_scores.astype(jnp.float32).reshape(HEADS, SIDE, SIDE, KS, KS)  156 us
    dynamic_slice x128, local copies, waits for them, and re-layouts, local(): lax.map(attend, (queries, keys_pooled, values_pooled, token_crop, key_crop))  129 us
    unnamed x13, waiting for transfers between devices  102 us
    dot_general x1, matrix products, local(): jnp.dot(normed_second, fc1_full, preferred_element_type=jnp.float32)  91.6 us
    unnamed x2, blocking collectives  90.5 us
    dot_general x32, matrix products, canvas_scores(): along_w = jnp.einsum('xyhd,ykd->hxyk', grid_q, rows_w, precision=highest)  90.3 us
    reduce_sum x16, other arithmetic, attend_back(): sum_w = jnp.sum(grid_grads, -2)  73.3 us
  transfers between devices with their start and end apart: 10, of which 2 were waited for; matrix products, arithmetic and copies ran while one was open for 55% of the time, Pallas kernels for 0%

commit v1 on v0

v1 whole, which is shorter than its diff:
```python
import jax
import jax.numpy as jnp
from jax import lax
from jax.experimental import pallas as pl
from jax.experimental.pallas import tpu as pltpu
from jax.sharding import PartitionSpec as P

D = 192
HEADS = 2
HD = 96
FF = 768
SIDE = 28
KS = 14
NTOK = 784
NKEY = 196
REL = 55

EPS = 1e-06
FILL = -1e30
LOG2E = 1.4426950408889634
LN2 = 0.6931471805599453
SCALE = HD ** (-0.5)
BASE = 32
KVROWS = BASE + NTOK + 24
bf = jnp.bfloat16
PAIR = 2
SKEW = 3
FEAT = 208
f32 = jnp.float32


def dot(a, b):
    return jnp.dot(a, b, preferred_element_type=f32)


def dot_nt(a, b):
    return lax.dot_general(a, b, (((1,), (1,)), ((), ())), preferred_element_type=f32)


def dot_tn(a, b):
    return lax.dot_general(a, b, (((0,), (0,)), ((), ())), preferred_element_type=f32)


def iota(shape, dim):
    return lax.broadcasted_iota(jnp.int32, shape, dim)


def widen(v):
    return jnp.concatenate([v, jnp.zeros((v.shape[0], 256 - v.shape[1]), v.dtype)], axis=1)


def lanes(col):
    return jnp.concatenate([col] * 6 + [col[:, :16]], axis=1)


def fold_lanes(v):
    total = v[:, 0:128]
    for n in range(1, 6):
        total = total + v[:, 128 * n:128 * n + 128]
    return total


def add_lanes(ref, tail, n, v):
    ref[n] += fold_lanes(v)
    tail[n] += v[:, 768:784]


def with_ones(v):
    extra = (iota((16, NTOK), 0) < 2).astype(f32).astype(bf)
    return jnp.concatenate([v, extra], 0)


def norm_cols(v):
    mean = jnp.sum(v, 0, keepdims=True) * (1.0 / D)
    c = v - mean
    var = jnp.sum(c * c, 0, keepdims=True) * (1.0 / D)
    r = lax.rsqrt(var + EPS)
    return c * r, r


def norm_cols_back(ge, u, r):
    s1 = jnp.sum(ge, 0, keepdims=True) * (1.0 / D)
    s2 = jnp.sum(ge * u, 0, keepdims=True) * (1.0 / D)
    return (ge - s1 - u * s2) * r


def fold(v):
    total = v[0:8]
    for n in range(1, v.shape[0] // 8):
        total = total + v[8 * n:8 * n + 8]
    return total


def norm_parts(v, mask, width):
    mean = jnp.sum(v, -1, keepdims=True) * (1.0 / width)
    c = (v - mean) * mask
    var = jnp.sum(c * c, -1, keepdims=True) * (1.0 / width)
    r = lax.rsqrt(var + EPS)
    return c * r, r


def norm_back(ge, u, r, width):
    s1 = jnp.sum(ge, -1, keepdims=True) * (1.0 / width)
    s2 = jnp.sum(ge * u, -1, keepdims=True) * (1.0 / width)
    return (ge - s1 - u * s2) * r


def roll_x(tile):
    out = []
    low = iota((8, 128), 0) < 4
    for p in range(KS):
        b = tile[56 * p:56 * p + 56]

        def by(v, n):
            return v if n == 0 else pltpu.roll(v, n, 1)

        out.append(by(b[0:24], 2 * p))
        out.append(jnp.where(low, by(b[24:32], 2 * p), by(b[24:32], 2 * p + 1)))
        out.append(by(b[32:56], 2 * p + 1))
    return out


def roll_y(tile):
    out = []
    low = iota((8, 128), 0) < 4
    for p in range(KS):
        b = tile[56 * p:56 * p + 56]
        out.append(pltpu.roll(b[0:24], 0, 1, stride=1, stride_axis=0))
        mid = b[24:32]
        first = pltpu.roll(mid, 24, 1, stride=1, stride_axis=0)
        second = pltpu.roll(pltpu.roll(mid, 124, 1), 0, 1, stride=1, stride_axis=0)
        out.append(jnp.where(low, first, second))
        out.append(pltpu.roll(b[32:56], 4, 1, stride=1, stride_axis=0))
    return out


def kernel(
    kc_ref, x_ref, g_ref, wq_ref, wqt_ref, wpt_ref, w1_ref, w1t_ref, w2_ref, w2t_ref,
    relf_ref, relb_ref, vec_ref, pk_ref, pv_ref,
    out_ref, ig_ref, gq_ref, gp_ref, g1_ref, g2_ref, grel_ref, gpk_ref, gpv_ref, gln_ref, tail_ref,
    kvs, gps, gkvs, kf, kb, vx,
):
    step = pl.program_id(0)

    @pl.when(step == 0)
    def _():
        for ref in (gq_ref, gp_ref, g1_ref, g2_ref, grel_ref, gpk_ref, gpv_ref, gln_ref, tail_ref):
            ref[...] = jnp.zeros_like(ref)
        kvs[...] = jnp.zeros_like(kvs)
        gps[...] = jnp.zeros_like(gps)
        key = iota((256, 128), 0)
        lane = iota((256, 128), 1)
        ki = key >> 4
        kj = key & 15
        spot = lane & 63
        low = lane < 64
        real = (kj < KS) & (ki < KS)
        for c, h in [(c, h) for c in range(PAIR) for h in range(HEADS)]:
            first, second = (ki, kj) if h == 0 else (kj, ki)
            which = jnp.where(low, first, second)
            kf[c, h, :, 128:] = jnp.where((spot == 27 + 2 * which) & real, 1.0, 0.0).astype(bf)
            kb[c, h, :, 128:] = jnp.where((spot == 26 - 2 * which) & real, 1.0, 0.0).astype(bf)
            kf[c, h, :, :128] = jnp.where((lane == HD) & (key >= 0), FILL, 0.0).astype(bf)
            kb[c, h, :, :128] = jnp.zeros((256, 128), bf)
            vx[c, h, :, :128] = jnp.zeros((256, 128), bf)
            vx[c, h, :, 128:] = jnp.ones((256, 128), bf)

    steps = [
        canvas(
            step * PAIR + c, c, kc_ref, x_ref, g_ref, wq_ref, wqt_ref, wpt_ref, w1_ref, w1t_ref, w2_ref, w2t_ref,
            relf_ref, relb_ref, vec_ref, pk_ref, pv_ref,
            out_ref, ig_ref, gq_ref, gp_ref, g1_ref, g2_ref, grel_ref, gpk_ref, gpv_ref, gln_ref, tail_ref,
            kvs.at[c], gps.at[c], gkvs.at[c], kf.at[c], kb.at[c], vx.at[c])
        for c in range(PAIR)]
    live = list(steps)
    started = 0
    tick = 0
    while live:
        for c, one in enumerate(steps):
            if one in live and tick >= c * SKEW:
                try:
                    next(one)
                except StopIteration:
                    live.remove(one)
        tick += 1


def canvas(
    item, slot, kc_ref, x_ref, g_ref, wq_ref, wqt_ref, wpt_ref, w1_ref, w1t_ref, w2_ref, w2t_ref,
    relf_ref, relb_ref, vec_ref, pk_ref, pv_ref,
    out_ref, ig_ref, gq_ref, gp_ref, g1_ref, g2_ref, grel_ref, gpk_ref, gpv_ref, gln_ref, tail_ref,
    kvs, gps, gkvs, kf, kb, vx,
):
    lane128 = iota((1, 128), 1)
    mask96 = (lane128 < HD).astype(f32)
    lowhalf = iota((NTOK, 128), 1) < 64

    gain1, shift1, gain2, shift2, fc2_bias = [lanes(vec_ref[n]) for n in range(5)]

    x = x_ref[slot].astype(f32)
    u1, r1 = norm_cols(x)
    nb = with_ones((u1 * gain1 + shift1).astype(bf))
    qb = dot_tn(nb, wq_ref[:, :256]).astype(bf)
    for n in range(4):
        kvs[n, BASE:BASE + NTOK, :] = dot_tn(nb, wq_ref[:, 256 + 128 * n:384 + 128 * n])

    yield
    notfirst = (iota((16, 128), 0) > 0).astype(f32)

    def tap(n, x_row, b):
        v = kvs.at[n][pl.ds(BASE + SIDE * x_row + b - 1, 16, stride=2), :]
        return v * notfirst if b == 0 else v

    u_pool, r_pool = [], []
    for n in range(4):
        w = n // 2
        rows = []
        for i in range(KS):
            acc = None
            for a in range(3):
                for b in range(3):
                    t = tap(n, 2 * i + a - 1, b) * pk_ref[w, 3 * a + b:3 * a + b + 1]
                    acc = t if acc is None else acc + t
            rows.append(acc)
        yield
        u, r = norm_parts(jnp.concatenate(rows, 0), mask96, HD)
        u_pool.append(u)
        r_pool.append(r)
        val = u * pv_ref[w:w + 1] + pv_ref[2 + w:3 + w]
        h = n % 2
        if w == 0:
            val = val * (SCALE * LOG2E)
            kb[h, 0:224, :128] = val.astype(bf)
            pad = ((iota((224, 128), 0) & 15) >= KS) & (iota((224, 128), 1) == HD)
            kf[h, 0:224, :128] = jnp.where(pad, FILL, val).astype(bf)
        else:
            vx[h, 0:224, :128] = val.astype(bf)

    yield
    row_cut = 0
    col_cut = 0
    for n in range(KS):
        row_cut = row_cut + jnp.where(kc_ref[item, KS * n] < 2, 2, 0)
        col_cut = col_cut + jnp.where((kc_ref[item, n] & 1) == 0, 2, 0)
    spot = (lane128 & 63) - 27
    row_side = spot >= row_cut
    col_side = spot >= col_cut
    rows_before = jnp.where(row_side, FILL, 0.0)
    rows_after = jnp.where(row_side, 0.0, FILL)
    y56 = iota((56, 128), 0)
    y56 = jnp.where(y56 >= SIDE, y56 - SIDE, y56)
    col_bias = jnp.where((y56 >= col_cut) != col_side, FILL, 0.0)

    a_h = dot(qb, relf_ref[:, :128])
    a_w = dot(qb, relf_ref[:, 128:])
    pieces_h = roll_x(a_h)
    pieces_w = roll_y(a_w)
    done_h, done_w = [], []
    for p in range(KS):
        row_bias = jnp.where(2 * p >= row_cut, rows_after, rows_before)
        done_h.append(jnp.concatenate(pieces_h[3 * p:3 * p + 3], 0) + row_bias)
        done_w.append(jnp.concatenate(pieces_w[3 * p:3 * p + 3], 0) + col_bias)
    t_h = jnp.concatenate(done_h, 0)
    t_w = jnp.concatenate(done_w, 0)
    rel = (jnp.where(lowhalf, t_h, t_w).astype(bf), jnp.where(lowhalf, t_w, t_h).astype(bf))

    yield
    eb, inv, mixed = [], [], []
    for h in range(HEADS):
        left = jnp.concatenate([qb[:, 128 * h:128 * h + 128], rel[h]], 1)
        s = dot_nt(left, kf[h])
        e = jnp.exp2(s - jnp.max(s, -1, keepdims=True)).astype(bf)
        yield
        o = dot(e, vx[h])
        rinv = 1.0 / o[:, 128:]
        eb.append(e)
        inv.append(rinv)
        mixed.append(o[:, :128] * rinv)
    ab = (jnp.concatenate(mixed, 1) + qb.astype(f32)).astype(bf)

    yield
    middle = x + dot_nt(wpt_ref[...], ab)
    u2, r2 = norm_cols(middle)
    n2b = with_ones((u2 * gain2 + shift2).astype(bf))
    gb = g_ref[slot]
    act, gh = [], []
    for n in range(3):
        cols = slice(256 * n, 256 * n + 256)
        hid = dot_tn(n2b, w1_ref[:, cols])
        phi = 0.5 * lax.erf(hid * 0.7071067811865476) + 0.5
        slope = phi + hid * jnp.exp2(hid * hid * (-0.5 * LOG2E)) * 0.3989422804014327
        yield
        act.append((hid * phi).astype(bf))
        gh.append((dot_tn(gb, w2t_ref[:, cols]) * slope).astype(bf))
    yield
    act = jnp.concatenate(act, 1)
    gh = jnp.concatenate(gh, 1)
    out = middle + fc2_bias + dot_nt(w2t_ref[...], act)
    out_ref[slot] = out.astype(bf)
    g2_ref[...] += dot(gb, act)
    g1_ref[...] += dot(n2b, gh)
    yield
    g = gb.astype(f32)
    add_lanes(gln_ref, tail_ref, 4, g)
    e2 = dot_nt(w1_ref[:D], gh)
    add_lanes(gln_ref, tail_ref, 2, e2 * u2)
    add_lanes(gln_ref, tail_ref, 3, e2)
    gm = g + norm_cols_back(e2 * gain2, u2, r2)
    grb = gm.astype(bf)
    gp_ref[...] += dot(grb, ab)
    yield
    gatt = dot_tn(grb, wpt_ref[...]).astype(bf).astype(f32)
    gr, gcont = [], []
    g2bs, dss = [], []
    for h in range(HEADS):
        ga = gatt[:, 128 * h:128 * h + 128]
        g2b = (ga * (inv[h] * LN2)).astype(bf)
        dd = jnp.sum(g2b.astype(f32) * mixed[h], -1, keepdims=True)
        yield
        gpr = dot_nt(g2b, vx[h, :, :128])
        ds = (eb[h].astype(f32) * (gpr - dd)).astype(bf)
        back = dot(ds, kb[h])
        gcont.append(back[:, :128])
        gr.append(back[:, 128:])
        dss.append(ds)
        g2bs.append(g2b)
    yield
    b_h = jnp.concatenate(roll_x(jnp.where(lowhalf, gr[0], gr[1])), 0)
    b_w = jnp.concatenate(roll_y(jnp.where(lowhalf, gr[1], gr[0])), 0)
    gab = jnp.concatenate([b_h, b_w], 1).astype(bf)
    gq = jnp.concatenate(gcont, 1) + dot(gab, relb_ref[...]) + gatt

    yield
    for n in range(4):
        w, h = n // 2, n % 2
        if w == 0:
            qt = dot_tn(qb[:, 128 * h:128 * h + 128], jnp.concatenate([dss[h], gab], 1))
            grel_ref[128 * h:128 * h + 128] += qt[:, 256:]
            e = jnp.transpose(qt[:, :256])[:224] * (SCALE * LOG2E)
        else:
            e = jnp.transpose(dot_tn(g2bs[h], eb[h]))[:224] * LOG2E
        yield
        gpv_ref[0, n] += fold(e * u_pool[n])
        gpv_ref[1, n] += fold(e)
        gps[n, 0:224, :] = norm_back(e * pv_ref[w:w + 1], u_pool[n], r_pool[n], HD)

    yield
    for n in range(4):
        w = n // 2
        for a in range(3):
            for b in range(3):
                acc = None
                for i in range(KS):
                    t = gps[n, 16 * i:16 * i + 16, :] * tap(n, 2 * i + a - 1, b)
                    acc = t if acc is None else acc + t
                gpk_ref[3 * a + b, n] += acc[0:8] + acc[8:16]

        yield

        def wk(a, b):
            return pk_ref[w, 3 * a + b:3 * a + b + 1]

        for i in range(KS):
            p0 = gps[n, 16 * i:16 * i + 16, :]
            p0s = gps[n, 16 * i + 1:16 * i + 17, :]
            p1 = gps[n, 16 * i + 16:16 * i + 32, :]
            p1s = gps[n, 16 * i + 17:16 * i + 33, :]
            even = SIDE * 2 * i
            odd = even + SIDE
            ee = p0 * wk(1, 1)
            eo = p0 * wk(1, 2) + p0s * wk(1, 0)
            oe = p0 * wk(2, 1) + p1 * wk(0, 1)
            oo = p0 * wk(2, 2) + p0s * wk(2, 0) + p1 * wk(0, 2) + p1s * wk(0, 0)
            gk = gkvs.at[n]
            gk[pl.ds(even, KS, stride=2), :] = ee[:KS]
            gk[pl.ds(even + 1, KS, stride=2), :] = eo[:KS]
            gk[pl.ds(odd, KS, stride=2), :] = oe[:KS]
            gk[pl.ds(odd + 1, KS, stride=2), :] = oo[:KS]

    yield
    gpk = jnp.concatenate([gq.astype(bf)] + [gkvs[n].astype(bf) for n in range(4)], 1)
    gq_ref[...] += dot(nb, gpk)
    e1 = dot_nt(wq_ref[:D], gpk)
    yield
    add_lanes(gln_ref, tail_ref, 0, e1 * u1)
    add_lanes(gln_ref, tail_ref, 1, e1)
    ig_ref[slot] = gm + norm_cols_back(e1 * gain1, u1, r1)


def pad_heads(v, groups):
    lead = v.shape[:-1]
    v = v.reshape(lead + (groups, HD))
    v = jnp.pad(v, ((0, 0),) * len(lead) + ((0, 0), (0, 128 - HD)))
    return v.reshape(lead + (groups * 128,))


def with_bias(weight, bias):
    hi = bias.astype(bf)
    lo = (bias - hi.astype(f32)).astype(bf)
    return jnp.concatenate([weight, hi[None], lo[None], jnp.zeros((14,) + bias.shape, bf)], 0)


def compute(
    block_input, key_crop, first_gain, first_bias, qkv_full, qkv_bias, pool_kernel, pool_gain,
    pool_bias, rel_height, rel_width, proj_full, proj_bias, second_gain, second_bias, fc1_full,
    fc1_bias, fc2_full, fc2_bias, cotangent,
):
    canvases = block_input.shape[0]
    spare = (jnp.arange(256) % 128 == HD).astype(f32)
    wq = with_bias(pad_heads(qkv_full, 6), pad_heads(qkv_bias, 6) + jnp.pad(spare, (0, 512)))
    wqt = pad_heads(qkv_full, 6).T
    proj_hi = proj_bias.astype(bf)
    proj_lo = (proj_bias - proj_hi.astype(f32)).astype(bf)
    wpt = pad_heads(proj_full.T, 2).at[:, HD].set(proj_hi).at[:, 128 + HD].set(proj_lo)
    w1 = with_bias(fc1_full, fc1_bias)
    w1t = fc1_full.T
    w2 = fc2_full
    w2t = fc2_full.T
    rel_h = jnp.pad(rel_height[:54] * LOG2E, ((0, 10), (0, 32)))
    rel_w = jnp.pad(rel_width[:54] * LOG2E, ((0, 10), (0, 32)))
    zero = jnp.zeros((64, 128), f32)
    relb = jnp.concatenate([
        jnp.concatenate([rel_h, zero], 1), jnp.concatenate([zero, rel_h], 1),
        jnp.concatenate([zero, rel_w], 1), jnp.concatenate([rel_w, zero], 1)], 0)
    flip_h = jnp.pad(rel_height[:54][::-1] * LOG2E, ((0, 10), (0, 32)))
    flip_w = jnp.pad(rel_width[:54][::-1] * LOG2E, ((0, 10), (0, 32)))
    relf = jnp.concatenate([
        jnp.concatenate([flip_h, zero], 1), jnp.concatenate([zero, flip_h], 1),
        jnp.concatenate([zero, flip_w], 1), jnp.concatenate([flip_w, zero], 1)], 0).T
    relb = relb.astype(bf)
    relf = relf.astype(bf)
    vec = jnp.broadcast_to(jnp.stack([first_gain, first_bias, second_gain, second_bias, fc2_bias])[..., None], (5, D, 128))
    pk = jnp.pad(pool_kernel, ((0, 0), (0, 0), (0, 32)))
    pv = jnp.pad(jnp.concatenate([pool_gain, pool_bias], 0), ((0, 0), (0, 32)))

    whole = lambda v: pl.BlockSpec(v.shape, lambda i, n=v.ndim: (0,) * n)
    per = lambda: pl.BlockSpec((PAIR, D, NTOK), lambda i: (i, 0, 0))
    consts = (wq, wqt, wpt, w1, w1t, w2, w2t, relf, relb, vec, pk, pv)
    sums = [(208, 768), (D, 256), (208, 768), (D, 768), (256, 256), (9, 4, 8, 128), (2, 4, 8, 128), (5, D, 128), (5, D, 16)]
    results = pl.pallas_call(
        kernel,
        grid=(canvases // PAIR,),
        in_specs=[pl.BlockSpec(memory_space=pltpu.SMEM), per(), per()] + [whole(v) for v in consts],
        out_specs=[per(), per()] + [pl.BlockSpec(s, lambda i, n=len(s): (0,) * n) for s in sums],
        out_shape=[jax.ShapeDtypeStruct((canvases, D, NTOK), bf), jax.ShapeDtypeStruct((canvases, D, NTOK), f32)]
        + [jax.ShapeDtypeStruct(s, f32) for s in sums],
        scratch_shapes=[
            pltpu.VMEM((PAIR, 4, KVROWS, 128), f32),
            pltpu.VMEM((PAIR, 4, 272, 128), f32),
            pltpu.VMEM((PAIR, 4, NTOK, 128), f32),
            pltpu.VMEM((PAIR, 2, 256, 256), bf),
            pltpu.VMEM((PAIR, 2, 256, 256), bf),
            pltpu.VMEM((PAIR, 2, 256, 256), bf),
        ],
        compiler_params=pltpu.CompilerParams(vmem_limit_bytes=60 * 2**20),
        name="block_step",
    )(key_crop, jnp.swapaxes(block_input, 1, 2), jnp.swapaxes(cotangent, 1, 2), *consts)
    out, ig, gq, gp, g1, g2, grel, gpk, gpv, gln, tail = results
    out = jnp.swapaxes(out, 1, 2)
    ig = jnp.swapaxes(ig, 1, 2)

    def unpad(v, groups):
        lead = v.shape[:-1]
        return v.reshape(lead + (groups, 128))[..., :HD].reshape(lead + (groups * HD,))

    gq_full = unpad(gq, 6)
    grad_qkv_weight, grad_qkv_bias = gq_full[:D], gq_full[D]
    grad_proj_weight = unpad(gp, 2).T
    grad_proj_bias = gp[:, HD]
    grad_fc1_weight, grad_fc1_bias = g1[:D], g1[D]
    grad_fc2_weight = g2.T
    h0, h1 = grel[:HD], grel[128:128 + HD]
    rel_pad = lambda v: jnp.pad(v.T[:54], ((0, 1), (0, 0))) * LOG2E
    grad_rel_height = rel_pad(h0[:, 0:64] + h1[:, 64:128])
    grad_rel_width = rel_pad(h0[:, 192:256] + h1[:, 128:192])
    gpk = gpk.sum(2)[..., :HD]
    grad_pool_kernel = jnp.stack([gpk[:, 0] + gpk[:, 1], gpk[:, 2] + gpk[:, 3]])
    gpv = gpv.sum(2)[..., :HD]
    grad_pool_gain = jnp.stack([gpv[0, 0] + gpv[0, 1], gpv[0, 2] + gpv[0, 3]])
    grad_pool_bias = jnp.stack([gpv[1, 0] + gpv[1, 1], gpv[1, 2] + gpv[1, 3]])
    gln = gln.sum(2) + tail.sum(2)
    return dict(
        out=out, ig=ig, qkv=grad_qkv_weight, proj=grad_proj_weight, fc1=grad_fc1_weight, fc2=grad_fc2_weight,
        small=(gln[0], gln[1], grad_qkv_bias, grad_pool_kernel, grad_pool_gain, grad_pool_bias,
               grad_rel_height, grad_rel_width, grad_proj_bias, gln[2], gln[3], grad_fc1_bias, gln[4]))


def gather_weights(shards):
    flat = jnp.concatenate([v.T.reshape(-1) for v in shards])
    every = lax.all_gather(flat, ("dp", "fsdp"), axis=0, tiled=False)
    dp, fsdp = lax.axis_size("dp"), lax.axis_size("fsdp")
    full = []
    start = 0
    for v in shards:
        rows, cols = v.shape
        part = every[:, start:start + rows * cols].reshape(dp, fsdp, cols, rows)
        full.append(jnp.transpose(part, (1, 3, 0, 2)).reshape(fsdp * rows, dp * cols))
        start += rows * cols
    return full


def reduce_weights(grads, shards):
    dp, fsdp = lax.axis_size("dp"), lax.axis_size("fsdp")
    parts = []
    for grad, v in zip(grads, shards):
        rows, cols = v.shape
        part = jnp.transpose(grad.astype(bf).reshape(fsdp, rows, dp, cols), (2, 0, 3, 1))
        parts.append(part.reshape(dp * fsdp, cols * rows))
    flat = jnp.concatenate(parts, 1)
    mine = lax.psum_scatter(flat, ("dp", "fsdp"), scatter_dimension=0, tiled=False).astype(f32)
    owned = []
    start = 0
    for v in shards:
        rows, cols = v.shape
        owned.append(mine[start:start + rows * cols].reshape(cols, rows).T)
        start += rows * cols
    return owned


def local(
    block_input, token_crop, key_crop, first_gain, first_bias, qkv_weight, qkv_bias, pool_kernel, pool_gain,
    pool_bias, rel_height, rel_width, proj_weight, proj_bias, second_gain, second_bias, fc1_weight, fc1_bias,
    fc2_weight, fc2_bias, cotangent,
):
    shards = (qkv_weight, proj_weight, fc1_weight, fc2_weight)
    qkv_full, proj_full, fc1_full, fc2_full = gather_weights(shards)
    r = compute(
        block_input, key_crop, first_gain, first_bias, qkv_full, qkv_bias, pool_kernel, pool_gain, pool_bias,
        rel_height, rel_width, proj_full, proj_bias, second_gain, second_bias, fc1_full, fc1_bias, fc2_full,
        fc2_bias, cotangent)
    owned = reduce_weights((r["qkv"], r["proj"], r["fc1"], r["fc2"]), shards)
    small = r["small"]
    flat = jnp.concatenate([v.reshape(-1) for v in small])
    flat = lax.psum(flat, ("dp", "fsdp"))
    summed = []
    start = 0
    for v in small:
        summed.append(flat[start:start + v.size].reshape(v.shape))
        start += v.size
    return (
        r["out"], r["ig"], summed[0], summed[1], owned[0], summed[2], summed[3], summed[4], summed[5], summed[6],
        summed[7], owned[1], summed[8], summed[9], summed[10], owned[2], summed[11], owned[3], summed[12])


def solution(mesh):
    rows = P(("dp", "fsdp"), None, None)
    ids = P(("dp", "fsdp"), None)
    block = P("fsdp", "dp")
    one = P()
    return jax.shard_map(
        local,
        mesh=mesh,
        in_specs=(rows, ids, ids, one, one, block, one, one, one, one, one, one, block, one, one, one, block, one,
                  block, one, rows),
        out_specs=(rows, rows, one, one, block, one, one, one, one, one, one, block, one, one, one, block, one,
                   block, one),
        check_vma=False,
    )
```

time: 3010 us -> 374 us (0.12)
  local copies, waits for them, and re-layouts: 1520 us -> 25.8 us
  matrix products: 825 us -> 0 us
  other arithmetic: 274 us -> 8.9 us
  Pallas kernels: 0 us -> 127 us
  blocking collectives: 234 us -> 117 us
    dot_general x260 -> x0, matrix products: 825 us -> none  [the longest x1 91.6 us: local(): jnp.dot(normed_second, fc1_full, preferred_element_type=jnp.float32)]
    add x146 -> x0, local copies, waits for them, and re-layouts: 721 us -> none  [the longest x128 696 us: canvas_scores(): content.reshape(HEADS, SIDE, SIDE, KS, KS) + along_h[..., :, None]]
    reshape x48 -> x33, local copies, waits for them, and re-layouts: 318 us -> 11.4 us  [the longest x4 3.08 us: gather_weights(): flat = jnp.concatenate([v.T.reshape(-1) for v in shards])]
    reduce_sum x45 -> x4, other arithmetic: 155 us -> 0.55 us  [the longest x2 0.48 us: compute(): gln = gln.sum(2) + tail.sum(2)]
    dynamic_slice x128 -> x0, local copies, waits for them, and re-layouts: 129 us -> none  [local(): lax.map(attend, (queries, keys_pooled, values_pooled, token_crop, key_crop))]
    pallas_call x0 -> x1, Pallas kernels: none -> 127 us  [compute(): pl.pallas_call(kernel, grid=(canvases // PAIR,), in_specs=[pl.BlockSpec(m...]
    unnamed x2 -> x0, blocking collectives: 90.5 us -> none
    unnamed x228 -> x57, local copies, waits for them, and re-layouts: 53.7 us -> 0.98 us
  transfers between devices with their start and end apart: 10 -> 1, of which waited for: 2 -> 1; matrix products, arithmetic and copies ran while one was open for 55% -> 2% of each run, Pallas kernels for 0% -> 0%
where the time goes in v1:
time: 374 us; the launch traced here: 373 us
  Pallas kernels  127 us (34%)
  blocking collectives  117 us (31%)
  waiting for transfers between devices  79.4 us (21%)
  local copies, waits for them, and re-layouts  25.8 us (7%)
  between operations  14.9 us (4%)
  other arithmetic  8.9 us (2%)
    pallas_call x1, Pallas kernels, compute(): pl.pallas_call(kernel, grid=(canvases // PAIR,), in_specs=[pl.BlockSpec(m...  127 us
    all_gather x1, blocking collectives, gather_weights(): every = lax.all_gather(flat, ('dp', 'fsdp'), axis=0, tiled=False)  79.5 us
    unnamed x2, waiting for transfers between devices  79.4 us
    psum x1, blocking collectives, local(): flat = lax.psum(flat, ('dp', 'fsdp'))  37.7 us
  transfers between devices with their start and end apart: 1, of which 1 were waited for; matrix products, arithmetic and copies ran while one was open for 2% of the time, Pallas kernels for 0%

profile of v1, /device:TPU:0, one launch (start us, length us, event | category | flops | bytes accessed | tf_op | source)
XLA Modules:
  0.0 373.0 jit_solution(7885959979479502936)
XLA Ops:
  7.2 0.6 compare_reduce_fusion.1
  7.9 0.6 compare_reduce_fusion
  8.5 0.8 reshape.367
  9.3 0.7 reshape.368
  10.0 0.8 reshape.365
  10.8 0.8 reshape.366
  11.7 79.5 %all-gather.1 = bf16[32,1,13824]{2,1,0:T(2,128)(2,1)S(1)} all-gather(bf16[1,1,13824]{2,1,0:T(2,128)(2,1)S(1)} %reshape.404), channel_id=2, replica_groups=mesh['dp'=16,'fsdp'=2] {'dp','fsdp'}, dimensions={0}, use_global_device_ids=true | all-gather | bytes 912384 | tf_op jit(solution)/shard_map/all_gather | solution.py:490
  94.9 0.9 copy.124.wq_ref
  96.4 0.9 copy.125.w2_ref
  97.4 0.8 copy.126.relf_ref
  98.2 0.7 slice_select_fusion.3
  99.2 0.8 slice_select_fusion.2
  100.2 0.7 fusion.16.relb_ref
  102.0 0.8 maximum_maximum_fusion.1.w1_ref
  102.9 1.0 broadcast_in_dim.23.vec_ref
  103.9 126.7 %block_step.1 = (bf16[16,192,784]{2,1,0:T(8,128)(2,1)}, f32[16,192,784]{2,1,0:T(8,128)}, f32[208,768]{1,0:T(8,128)}, f32[192,256]{1,0:T(8,128)}, f32[208,768]{1,...) custom-call(s32[16,196]{1,0:T(8,128)} %kc_ref.1, ...), custom_call_target="tpu_custom_call" | custom-call | tf_op jit(solution)/shard_map/block_step/pallas_call | solution.py:440
  230.6 1.2 reshape.383
  232.6 1.1 slice.420
  235.4 1.0 pad_maximum_fusion
  236.4 0.8 slice_reduce_fusion.4
  239.0 37.7 %psum.7 = f32[15168]{0:T(1024)S(1)} all-reduce(f32[15168]{0:T(1024)S(1)} %concatenate.68), channel_id=1, replica_groups=mesh['dp'=16,'fsdp'=2] {'dp','fsdp'}, use_global_device_ids=true, to_apply=%region_6.7 | all-reduce | flops 15168 | bytes 121344 | tf_op jit(solution)/shard_map/psum | solution.py:534
  278.0 0.7 reshape.400
  278.7 0.7 reshape.401
  280.0 0.6 fusion.29
  280.7 0.6 reshape.398
  281.3 0.6 reshape.399
  282.0 79.4 %all-reduce.21.cloned.1.call-done = bf16[32,13824]{1,0:T(8,128)(2,1)} async-done(((bf16[32,13824]{1,0:T(8,128)(2,1)}), bf16[32,13824]{1,0:T(8,128)(2,1)}) %all-reduce.21.cloned.1.call-update) | async-done | bytes 884752
  361.4 1.0 dynamic-slice_convert_fusion
  362.5 0.7 slice.324
  363.1 0.7 slice.311
  363.8 0.7 slice.319
  364.5 1.0 fusion.19
  (156 shorter events, 12.5 us)
Async XLA Ops:
  7.2 354.2 %all-reduce.21.cloned.1.call-start = ((), (), s32[]{:S(2)}) async-start(), calls=%async_computation | async-start | bytes 1769472
  91.3 0.7 copy-start.16
  91.8 1.3 copy-start.14
  92.9 1.6 copy-start
  92.9 1.1 copy-start.15
  94.1 2.1 copy-start.1
  94.8 2.4 copy-start.10
  94.9 2.5 copy-start.11
  95.8 2.4 copy-start.13
  96.0 5.5 %copy-start.17 = (f32[2,96]{1,0:T(2,128)S(1)}, f32[2,96]{1,0:T(2,128)}, u32[]{:S(2)}) copy-start(f32[2,96]{1,0:T(2,128)} %param.33) | copy-start | bytes 2308
  96.0 5.5 %copy-start.18 = (f32[2,96]{1,0:T(2,128)S(1)}, f32[2,96]{1,0:T(2,128)}, u32[]{:S(2)}) copy-start(f32[2,96]{1,0:T(2,128)} %param.32) | copy-start | bytes 2308
  96.2 6.7 %copy-start.19 = (f32[192]{0:T(256)S(1)}, f32[192]{0:T(256)}, u32[]{:S(2)}) copy-start(f32[192]{0:T(256)} %param.27) | copy-start | bytes 2308
  96.3 6.6 %copy-start.20 = (f32[192]{0:T(256)S(1)}, f32[192]{0:T(256)}, u32[]{:S(2)}) copy-start(f32[192]{0:T(256)} %param.28) | copy-start | bytes 2308
  96.3 6.6 %copy-start.21 = (f32[192]{0:T(256)S(1)}, f32[192]{0:T(256)}, u32[]{:S(2)}) copy-start(f32[192]{0:T(256)} %param.38) | copy-start | bytes 2308
  96.3 6.6 %copy-start.22 = (f32[192]{0:T(256)S(1)}, f32[192]{0:T(256)}, u32[]{:S(2)}) copy-start(f32[192]{0:T(256)} %param.39) | copy-start | bytes 2308
  96.3 6.6 %copy-start.23 = (f32[192]{0:T(256)S(1)}, f32[192]{0:T(256)}, u32[]{:S(2)}) copy-start(f32[192]{0:T(256)} %param.43) | copy-start | bytes 2308
  96.3 7.6 %copy-start.2 = (bf16[24,8,2,384]{3,1,2,0:T(8,128)(2,1)}, bf16[24,8,2,384]{3,1,2,0:T(8,128)(2,1)S(1)}, u32[]{:S(2)}) copy-start(bf16[24,8,2,384]{3,1,2,0:T(8,128)(2,1)S(1)} %copy.151) | copy-start | bytes 884740
  100.2 3.8 %copy-start.3 = (bf16[192,256]{1,0:T(8,128)(2,1)}, bf16[192,256]{1,0:T(8,128)(2,1)S(1)}, u32[]{:S(2)}) copy-start(bf16[192,256]{1,0:T(8,128)(2,1)S(1)} %scatter.9.wpt_ref) | copy-start | bytes 294916
  232.6 2.0 copy-start.7
  233.9 1.2 copy-start.4
  235.2 2.1 copy-start.12
  235.2 2.3 copy-start.6
  235.3 2.5 copy-start.5
  235.3 2.8 copy-start.8
  235.3 2.9 copy-start.24
  236.3 2.3 copy-start.9
Sparse Core Ops, SparseCore 0:
  236.5 124.8 all-reduce.20

commit v2 on v1

--- a/solution.py
+++ b/solution.py
@@ -1,3 +1,5 @@
+import functools
+
 import jax
 import jax.numpy as jnp
 from jax import lax
@@ -135,9 +137,10 @@
 
 
 def kernel(
-    kc_ref, x_ref, g_ref, wq_ref, wqt_ref, wpt_ref, w1_ref, w1t_ref, w2_ref, w2t_ref,
+    wire, kc_ref, x_ref, g_ref, wq_ref, wpt_ref, w1_ref, w2t_ref,
     relf_ref, relb_ref, vec_ref, pk_ref, pv_ref,
-    out_ref, ig_ref, gq_ref, gp_ref, g1_ref, g2_ref, grel_ref, gpk_ref, gpv_ref, gln_ref, tail_ref,
+    out_ref, ig_ref, wire_ref, small_ref,
+    gq_ref, gp_ref, g1_ref, g2_ref, grel_ref, gpk_ref, gpv_ref, gln_ref, tail_ref, table, piece,
     kvs, gps, gkvs, kf, kb, vx,
 ):
     step = pl.program_id(0)
@@ -167,7 +170,7 @@
 
     steps = [
         canvas(
-            step * PAIR + c, c, kc_ref, x_ref, g_ref, wq_ref, wqt_ref, wpt_ref, w1_ref, w1t_ref, w2_ref, w2t_ref,
+            step * PAIR + c, c, kc_ref, x_ref, g_ref, wq_ref, wpt_ref, w1_ref, w2t_ref,
             relf_ref, relb_ref, vec_ref, pk_ref, pv_ref,
             out_ref, ig_ref, gq_ref, gp_ref, g1_ref, g2_ref, grel_ref, gpk_ref, gpv_ref, gln_ref, tail_ref,
             kvs.at[c], gps.at[c], gkvs.at[c], kf.at[c], kb.at[c], vx.at[c])
@@ -184,9 +187,59 @@
                     live.remove(one)
         tick += 1
 
+    @pl.when(step == pl.num_programs(0) - 1)
+    def _():
+        pack(wire, wire_ref, small_ref, gq_ref, gp_ref, g1_ref, g2_ref, grel_ref, gpk_ref, gpv_ref, gln_ref,
+             tail_ref, table, piece)
+
+
+def pack(wire, wire_ref, small_ref, gq_ref, gp_ref, g1_ref, g2_ref, grel_ref, gpk_ref, gpv_ref, gln_ref, tail_ref,
+         table, piece):
+    wide = wire.width
+    for g in range(6):
+        table[HD * g:HD * g + HD, :] = jnp.transpose(gq_ref[:D, 128 * g:128 * g + 128])[:HD]
+    table[3 * D:4 * D, :] = jnp.concatenate([gp_ref[:, 0:HD], gp_ref[:, 128:128 + HD]], 1)
+    table[4 * D:4 * D + FF, :] = jnp.transpose(g1_ref[:D])
+    piece[...] = jnp.zeros_like(piece)
+    for d in range(wire.dp):
+        for first, count, at in wire.starts(d):
+            piece[first:first + count, :] = table[at:at + count, :]
+        low = g2_ref[wire.low * d:wire.low * (d + 1), :]
+        for f in range(wire.fsdp):
+            for q in range(wire.parts):
+                first = wire.top + q * wire.low
+                at = (f * wire.parts + q) * wide
+                piece[first:first + wire.low, f * wide:(f + 1) * wide] = low[:, at:at + wide]
+        for f in range(wire.fsdp):
+            part = piece[:, f * wide:(f + 1) * wide]
+            part = jnp.concatenate([part, jnp.zeros((wire.pad, 128 - wide), f32)], 1)
+            wire_ref[wire.slot(d, f)] = part.astype(bf)
+    small_ref[...] = jnp.zeros_like(small_ref)
+    turned = jnp.transpose(grel_ref[...]) * LOG2E
+    small_ref[0:64] = turned[0:64, 0:128] + turned[64:128, 128:256]
+    small_ref[64:128] = turned[192:256, 0:128] + turned[128:192, 128:256]
+    for w in range(2):
+        for k in range(9):
+            small_ref[128 + 9 * w + k:129 + 9 * w + k] = jnp.sum(
+                gpk_ref[k, 2 * w] + gpk_ref[k, 2 * w + 1], 0, keepdims=True)
+        for m in range(2):
+            small_ref[146 + 2 * m + w:147 + 2 * m + w] = jnp.sum(
+                gpv_ref[m, 2 * w] + gpv_ref[m, 2 * w + 1], 0, keepdims=True)
+    for g in range(6):
+        small_ref[152 + g:153 + g] = gq_ref[D:D + 1, 128 * g:128 * g + 128]
+        small_ref[158 + g:159 + g] = g1_ref[D:D + 1, 128 * g:128 * g + 128]
+    rows = []
+    for k in range(5):
+        rows.append(jnp.sum(jnp.transpose(gln_ref[k]), 0, keepdims=True)
+                    + jnp.sum(jnp.transpose(tail_ref[k]), 0, keepdims=True))
+    rows.append(jnp.transpose(gp_ref[:, 0:128])[HD:HD + 1])
+    for k, v in enumerate(rows):
+        small_ref[164 + 2 * k:165 + 2 * k] = v[:, 0:128]
+        small_ref[165 + 2 * k:166 + 2 * k] = jnp.concatenate([v[:, 128:D], jnp.zeros((1, 256 - D), f32)], 1)
+
 
 def canvas(
-    item, slot, kc_ref, x_ref, g_ref, wq_ref, wqt_ref, wpt_ref, w1_ref, w1t_ref, w2_ref, w2t_ref,
+    item, slot, kc_ref, x_ref, g_ref, wq_ref, wpt_ref, w1_ref, w2t_ref,
     relf_ref, relb_ref, vec_ref, pk_ref, pv_ref,
     out_ref, ig_ref, gq_ref, gp_ref, g1_ref, g2_ref, grel_ref, gpk_ref, gpv_ref, gln_ref, tail_ref,
     kvs, gps, gkvs, kf, kb, vx,
@@ -387,64 +440,394 @@
     ig_ref[slot] = gm + norm_cols_back(e1 * gain1, u1, r1)
 
 
-def pad_heads(v, groups):
-    lead = v.shape[:-1]
-    v = v.reshape(lead + (groups, HD))
-    v = jnp.pad(v, ((0, 0),) * len(lead) + ((0, 0), (0, 128 - HD)))
-    return v.reshape(lead + (groups * 128,))
-
-
-def with_bias(weight, bias):
-    hi = bias.astype(bf)
-    lo = (bias - hi.astype(f32)).astype(bf)
-    return jnp.concatenate([weight, hi[None], lo[None], jnp.zeros((14,) + bias.shape, bf)], 0)
-
-
-def compute(
-    block_input, key_crop, first_gain, first_bias, qkv_full, qkv_bias, pool_kernel, pool_gain,
-    pool_bias, rel_height, rel_width, proj_full, proj_bias, second_gain, second_bias, fc1_full,
-    fc1_bias, fc2_full, fc2_bias, cotangent,
+MESH = pl.DeviceIdType.MESH
+
+
+class Wire:
+    def __init__(self, dp, fsdp):
+        self.dp, self.fsdp, self.n = dp, fsdp, dp * fsdp
+        self.chips = self.n // 2
+        self.rows = (3 * D // dp, D // dp, FF // dp)
+        self.top = sum(self.rows)
+        self.low = D // dp
+        self.width = D // fsdp
+        self.parts = FF // fsdp // self.width
+        self.used = self.top + self.parts * self.low
+        self.pad = -(-self.used // 16) * 16
+
+    def starts(self, d):
+        a, b, c = self.rows
+        return ((0, a, a * d), (a, b, 3 * D + b * d), (a + b, c, 4 * D + c * d))
+
+    def slot(self, d, f):
+        return (d % 2) * self.chips + (d // 2) * self.fsdp + f
+
+    def place(self):
+        d, f = lax.axis_index("dp"), lax.axis_index("fsdp")
+        core = lax.rem(d, 2)
+        return core, (d // 2) * self.fsdp + f
+
+    def device(self, core, chip):
+        return (2 * (chip // self.fsdp) + core, lax.rem(chip, self.fsdp))
+
+
+def gather_kernel(
+    wire, qkv, proj, fc1, fc2, qkv_bias, proj_bias, fc1_bias, gain1, shift1, gain2, shift2, fc2_bias,
+    pool_kernel, pool_gain, pool_bias, rel_h, rel_w,
+    wq_ref, wpt_ref, w1_ref, w2t_ref, relf_ref, relb_ref, vec_ref, pk_ref, pv_ref,
+    buf, mine, tmp, table, low_table, send, forward, recv,
 ):
+    n, nc = wire.n, wire.chips
+    core, chip = wire.place()
+    other = 1 - core
+    partner = wire.device(other, chip)
+    me = core * nc + chip
+    barrier = pltpu.get_barrier_semaphore()
+    pl.semaphore_signal(barrier, inc=1, device_id=partner, device_id_type=MESH)
+
+    def greet(k, c):
+        pl.semaphore_signal(barrier, inc=1, device_id=wire.device(core, lax.rem(chip + k, nc)), device_id_type=MESH)
+        return c
+
+    lax.fori_loop(1, nc, greet, 0)
+
+    wide = wire.width
+    a, b, c = wire.rows
+    tmp[...] = jnp.zeros_like(tmp)
+    tmp[0:a, :wide] = qkv[...].astype(f32)
+    tmp[a:a + b, :wide] = proj[...].astype(f32)
+    tmp[a + b:wire.top, :wide] = fc1[...].astype(f32)
+    below = fc2[...].astype(f32)
+    for q in range(wire.parts):
+        first = wire.top + q * wire.low
+        tmp[first:first + wire.low, :wide] = below[:, q * wide:(q + 1) * wide]
+    mine[...] = tmp[:, :128].astype(bf)
+    pl.semaphore_wait(barrier, nc)
+
+    def to_partner(src, slot, k):
+        return pltpu.make_async_remote_copy(
+            src_ref=src, dst_ref=buf.at[slot], send_sem=forward.at[k], recv_sem=recv.at[slot],
+            device_id=partner, device_id_type=MESH)
+
+    def to_chip(k):
+        return pltpu.make_async_remote_copy(
+            src_ref=mine, dst_ref=buf.at[me], send_sem=send.at[k], recv_sem=recv.at[me],
+            device_id=wire.device(core, lax.rem(chip + k, nc)), device_id_type=MESH)
+
+    def start(k, c):
+        to_chip(nc - k).start()
+        return c
+
+    lax.fori_loop(1, nc, start, 0)
+    to_partner(mine, me, 0).start()
+
+    def row(ref):
+        return ref[...].reshape(1, ref.shape[0])
+
+    for k, ref in enumerate((gain1, shift1, gain2, shift2, fc2_bias)):
+        vec_ref[k] = jnp.transpose(jnp.broadcast_to(row(ref), (128, D)))
+    zero32 = jnp.zeros((64, 128 - HD), f32)
+
+    def tall(ref):
+        t = jnp.concatenate([ref[...] * LOG2E, jnp.zeros((64 - REL, HD), f32)], 0)
+        t = jnp.concatenate([t, zero32], 1)
+        return jnp.where(iota((64, 128), 0) < 54, t, 0.0)
+
+    th, tw = tall(rel_h), tall(rel_w)
+    none = jnp.zeros((64, 128), f32)
+    relb = jnp.concatenate([
+        jnp.concatenate([th, none], 1), jnp.concatenate([none, th], 1),
+        jnp.concatenate([none, tw], 1), jnp.concatenate([tw, none], 1)], 0).astype(bf)
+    relb_ref[...] = relb
+    at, to = iota((256, 256), 0), iota((256, 256), 1)
+    mirror = ((at >> 6) == (to >> 6)) & ((at & 63) + (to & 63) == 53)
+    relf_ref[...] = dot_tn(relb, jnp.where(mirror, 1.0, 0.0).astype(bf)).astype(bf)
+    for w in range(2):
+        taps = jnp.concatenate([pool_kernel[k, w:w + 1, :] for k in range(9)], 0)
+        pk_ref[w] = jnp.concatenate([taps, jnp.zeros((9, 128 - HD), f32)], 1)
+    four = jnp.concatenate([pool_gain[...], pool_bias[...]], 0)
+    pv_ref[...] = jnp.concatenate([four, jnp.zeros((4, 128 - HD), f32)], 1)
+
+    def relay(k, c):
+        slot = core * nc + lax.rem(chip + k, nc)
+        pltpu.make_async_remote_copy(
+            src_ref=mine, dst_ref=buf.at[slot], send_sem=send.at[0], recv_sem=recv.at[slot],
+            device_id=partner, device_id_type=MESH).wait_recv()
+        to_partner(buf.at[slot], slot, k).start()
+        return c
+
+    lax.fori_loop(1, nc, relay, 0)
+
+    def arrive(k, c):
+        to_partner(mine, other * nc + k, 0).wait_recv()
+        return c
+
+    lax.fori_loop(0, nc, arrive, 0)
+    buf[pl.ds(me, 1)] = mine[...][None]
+
+    for d in range(wire.dp):
+        blocks = [buf[wire.slot(d, f)].astype(f32) for f in range(wire.fsdp)]
+        tmp[...] = jnp.concatenate([v[:, :wide] for v in blocks], 1)
+        for first, count, to_row in wire.starts(d):
+            table[to_row:to_row + count, :] = tmp[first:first + count, :]
+        for f in range(wire.fsdp):
+            parts = [tmp[wire.top + q * wire.low:wire.top + (q + 1) * wire.low, f * wide:(f + 1) * wide]
+                     for q in range(wire.parts)]
+            low_table[wire.low * d:wire.low * (d + 1), f * wide * wire.parts:(f + 1) * wide * wire.parts] = (
+                jnp.concatenate(parts, 1))
+
+    def two(bias):
+        hi = bias.astype(bf).astype(f32)
+        return jnp.concatenate([hi, bias - hi, jnp.zeros((14, bias.shape[1]), f32)], 0)
+
+    qb = row(qkv_bias)
+    for g in range(6):
+        block = jnp.concatenate([jnp.transpose(table[HD * g:HD * g + HD, :]), two(qb[:, HD * g:HD * g + HD])], 0)
+        spare = (iota((FEAT, 128 - HD), 0) == D) & (iota((FEAT, 128 - HD), 1) == 0) & (g < 2)
+        block = jnp.concatenate([block, jnp.where(spare, 1.0, 0.0)], 1)
+        wq_ref[:, 128 * g:128 * g + 128] = block.astype(bf)
+    cols = []
+    pb = row(proj_bias)
+    hi = pb.astype(bf).astype(f32)
+    for g, extra in enumerate((hi, pb - hi)):
+        col = jnp.transpose(jnp.broadcast_to(extra, (128, D)))[:, :128 - HD]
+        col = jnp.where(iota((D, 128 - HD), 1) == 0, col, 0.0)
+        cols += [table[3 * D:4 * D, HD * g:HD * g + HD], col]
+    wpt_ref[...] = jnp.concatenate(cols, 1).astype(bf)
+    w1_ref[...] = jnp.concatenate([jnp.transpose(table[4 * D:4 * D + FF, :]), two(row(fc1_bias))], 0).astype(bf)
+    w2t_ref[...] = low_table[...].astype(bf)
+
+    def finish(k, c):
+        to_chip(k).wait_send()
+        to_partner(mine, me, k).wait_send()
+        return c
+
+    lax.fori_loop(1, nc, finish, 0)
+    to_partner(mine, me, 0).wait_send()
+
+
+def staged(body, ins, outs, *refs):
+    a, b = len(ins), len(outs)
+    src, dst = refs[:a], refs[a:a + b]
+    vin, vout = refs[a + b:2 * a + b], refs[2 * a + b:2 * (a + b)]
+    sems, rest = refs[2 * (a + b)], refs[2 * (a + b) + 1:]
+    loads = [pltpu.make_async_copy(s, v, sems.at[k]) for k, (s, v) in enumerate(zip(src, vin))]
+    for c in loads:
+        c.start()
+    for c in loads:
+        c.wait()
+    body(*vin, *vout, *rest)
+    stores = [pltpu.make_async_copy(v, d, sems.at[k]) for k, (v, d) in enumerate(zip(vout, dst))]
+    for c in stores:
+        c.start()
+    for c in stores:
+        c.wait()
+
+
+def staged_call(body, args, shapes, scratch, **params):
+    hbm = pl.BlockSpec(memory_space=pltpu.HBM)
+    ins = [(v.shape, v.dtype) for v in args]
+    name = params.pop("name")
+    return pl.pallas_call(
+        functools.partial(staged, body, ins, shapes),
+        in_specs=[hbm] * len(ins),
+        out_specs=[hbm] * len(shapes),
+        out_shape=[jax.ShapeDtypeStruct(*s) for s in shapes],
+        scratch_shapes=[pltpu.VMEM(*s) for s in ins + list(shapes)]
+        + [pltpu.SemaphoreType.DMA((max(len(ins), len(shapes)),))] + list(scratch),
+        compiler_params=pltpu.CompilerParams(**params),
+        name=name,
+    )(*args)
+
+
+def gather(wire, shards, vectors):
+    shapes = [((FEAT, FF), bf), ((D, 256), bf), ((FEAT, FF), bf), ((D, FF), bf), ((256, 256), bf), ((256, 256), bf),
+              ((5, D, 128), f32), ((2, 9, 128), f32), ((4, 128), f32)]
+    args = [v.T for v in shards] + list(vectors)
+    scratch = [
+        pltpu.VMEM((wire.n, wire.pad, 128), bf),
+        pltpu.VMEM((wire.pad, 128), bf),
+        pltpu.VMEM((wire.pad, D), f32),
+        pltpu.VMEM((4 * D + FF, D), f32),
+        pltpu.VMEM((D, FF), f32),
+        pltpu.SemaphoreType.DMA((wire.chips,)),
+        pltpu.SemaphoreType.DMA((wire.chips,)),
+        pltpu.SemaphoreType.DMA((wire.n,)),
+    ]
+    return staged_call(
+        functools.partial(gather_kernel, wire), args, shapes, scratch,
+        vmem_limit_bytes=60 * 2**20, collective_id=0, has_side_effects=True, name="gather_weights")
+
+
+def reduce_kernel(
+    wire, grads, small, res_ref, sum_ref,
+    abuf, comb, bbuf, sbuf, own, gsm, asend, arecv, bsend, brecv, ssend, srecv, gsend, grecv,
+):
+    n, nc = wire.n, wire.chips
+    core, chip = wire.place()
+    other = 1 - core
+    partner = wire.device(other, chip)
+    me = core * nc + chip
+    barrier = pltpu.get_barrier_semaphore()
+
+    def peer(k):
+        slot = lax.rem(me + k, n)
+        return slot, wire.device(slot // nc, lax.rem(slot, nc))
+
+    def greet(k, c):
+        pl.semaphore_signal(barrier, inc=1, device_id=peer(k)[1], device_id_type=MESH)
+        return c
+
+    lax.fori_loop(1, n, greet, 0)
+    pl.semaphore_wait(barrier, n - 1)
+
+    def half(k):
+        to = lax.rem(chip + k, nc)
+        return pltpu.make_async_remote_copy(
+            src_ref=grads.at[other * nc + to], dst_ref=abuf.at[to], send_sem=asend.at[k], recv_sem=arecv.at[to],
+            device_id=partner, device_id_type=MESH)
+
+    def little(k):
+        slot, device = peer(k)
+        return pltpu.make_async_remote_copy(
+            src_ref=small.at[slot], dst_ref=sbuf.at[n - 1 - k], send_sem=ssend.at[k], recv_sem=srecv,
+            device_id=device, device_id_type=MESH)
+
+    def spread(k):
+        slot, device = peer(k)
+        return pltpu.make_async_remote_copy(
+            src_ref=own, dst_ref=gsm.at[n - 1 - k], send_sem=gsend.at[k], recv_sem=grecv,
+            device_id=device, device_id_type=MESH)
+
+    def piece(k):
+        to = lax.rem(chip + k, nc)
+        return pltpu.make_async_remote_copy(
+            src_ref=comb.at[to], dst_ref=bbuf.at[nc - 1 - k], send_sem=bsend.at[k], recv_sem=brecv,
+            device_id=wire.device(core, to), device_id_type=MESH)
+
+    def loop(lo, hi, fn):
+        def body(k, c):
+            fn(k)
+            return c
+        lax.fori_loop(lo, hi, body, 0)
+
+    loop(1, n, lambda k: little(k).start())
+    loop(0, nc, lambda k: half(lax.rem(k + 1, nc)).start())
+
+    def merge(k):
+        to = lax.rem(chip + k, nc)
+        half(k).wait_recv()
+        comb[pl.ds(to, 1)] = (grads[pl.ds(core * nc + to, 1)].astype(f32) + abuf[pl.ds(to, 1)].astype(f32)).astype(bf)
+
+    def forward(k):
+        merge(k)
+        piece(k).start()
+
+    loop(1, nc, forward)
+    merge(0)
+
+    pltpu.make_async_copy(sbuf, sbuf, srecv).wait()
+    total = small[pl.ds(me, 1)][0]
+    for k in range(n - 1):
+        total = total + sbuf[k]
+    own[...] = total
+    loop(1, n, lambda k: spread(k).start())
+
+    pltpu.make_async_copy(bbuf, bbuf, brecv).wait()
+    total = comb[pl.ds(chip, 1)][0].astype(f32)
+    for k in range(nc - 1):
+        total = total + bbuf[k].astype(f32)
+    res_ref[...] = total
+
+    pltpu.make_async_copy(gsm, gsm, grecv).wait()
+    sum_ref[pl.ds(me, 1)] = own[...][None]
+
+    def keep(k):
+        sum_ref[pl.ds(lax.rem(me + n - k, n), 1)] = gsm[pl.ds(n - 1 - k, 1)]
+
+    loop(1, n, keep)
+    loop(0, nc, lambda k: half(k).wait_send())
+
+    def done(k):
+        little(k).wait_send()
+        spread(k).wait_send()
+
+    loop(1, n, done)
+    loop(1, nc, lambda k: piece(k).wait_send())
+
+
+def reduce(wire, grads, small):
+    n, nc = wire.n, wire.chips
+    dma = pltpu.SemaphoreType.DMA
+    scratch = [
+        pltpu.VMEM((nc, wire.pad, 128), bf),
+        pltpu.VMEM((nc, wire.pad, 128), bf),
+        pltpu.VMEM((nc - 1, wire.pad, 128), bf),
+        pltpu.VMEM((n - 1, 8, 128), f32),
+        pltpu.VMEM((8, 128), f32),
+        pltpu.VMEM((n - 1, 8, 128), f32),
+        dma((nc,)), dma((nc,)), dma((nc,)), dma, dma((n,)), dma, dma((n,)), dma,
+    ]
+    return staged_call(
+        functools.partial(reduce_kernel, wire), (grads, small), [((wire.pad, 128), f32), ((n, 8, 128), f32)], scratch,
+        vmem_limit_bytes=60 * 2**20, collective_id=1, has_side_effects=True, name="reduce_gradients")
+
+
+def finish_kernel(
+    wire, res, rows, qkv, proj, fc1, fc2, qkv_bias, proj_bias, fc1_bias, gain1, shift1, gain2, shift2, fc2_bias,
+    pool_kernel, pool_gain, pool_bias, rel_h, rel_w,
+):
+    wide = wire.width
+    a, b, c = wire.rows
+    qkv[...] = res[0:a, :wide]
+    proj[...] = res[a:a + b, :wide]
+    fc1[...] = res[a + b:wire.top, :wide]
+    fc2[...] = jnp.concatenate(
+        [res[wire.top + q * wire.low:wire.top + (q + 1) * wire.low, :wide] for q in range(wire.parts)], 1)
+    rel_h[...] = rows[0:REL, :HD]
+    rel_w[...] = rows[64:64 + REL, :HD]
+    for k in range(9):
+        for w in range(2):
+            pool_kernel[k, w:w + 1, :] = rows[128 + 9 * w + k:129 + 9 * w + k, :HD]
+    pool_gain[...] = rows[146:148, :HD]
+    pool_bias[...] = rows[148:150, :HD]
+    at = 152
+    qkv_bias[...] = jnp.concatenate([rows[at + g:at + g + 1, :HD] for g in range(6)], 1).reshape(3 * D)
+    at = 158
+    fc1_bias[...] = jnp.concatenate([rows[at + g:at + g + 1, :] for g in range(6)], 1).reshape(FF)
+    at = 164
+    for k, ref in enumerate((gain1, shift1, gain2, shift2, fc2_bias, proj_bias)):
+        first = at + 2 * k
+        ref[...] = jnp.concatenate([rows[first:first + 1, :], rows[first + 1:first + 2, :D - 128]], 1).reshape(D)
+
+
+def finish(wire, res, rows):
+    a, b, c = wire.rows
+    wide = wire.width
+    shapes = [(a, wide), (b, wide), (c, wide), (wire.low, wire.parts * wide), (3 * D,), (D,), (FF,)]
+    shapes += [(D,)] * 5 + [(9, 2, HD), (2, HD), (2, HD), (REL, HD), (REL, HD)]
+    return staged_call(
+        functools.partial(finish_kernel, wire), (res, rows.reshape(-1, 128)), [(v, f32) for v in shapes], [],
+        vmem_limit_bytes=60 * 2**20, name="split_gradients")
+
+
+def compute(wire, block_input, key_crop, cotangent, consts):
     canvases = block_input.shape[0]
-    spare = (jnp.arange(256) % 128 == HD).astype(f32)
-    wq = with_bias(pad_heads(qkv_full, 6), pad_heads(qkv_bias, 6) + jnp.pad(spare, (0, 512)))
-    wqt = pad_heads(qkv_full, 6).T
-    proj_hi = proj_bias.astype(bf)
-    proj_lo = (proj_bias - proj_hi.astype(f32)).astype(bf)
-    wpt = pad_heads(proj_full.T, 2).at[:, HD].set(proj_hi).at[:, 128 + HD].set(proj_lo)
-    w1 = with_bias(fc1_full, fc1_bias)
-    w1t = fc1_full.T
-    w2 = fc2_full
-    w2t = fc2_full.T
-    rel_h = jnp.pad(rel_height[:54] * LOG2E, ((0, 10), (0, 32)))
-    rel_w = jnp.pad(rel_width[:54] * LOG2E, ((0, 10), (0, 32)))
-    zero = jnp.zeros((64, 128), f32)
-    relb = jnp.concatenate([
-        jnp.concatenate([rel_h, zero], 1), jnp.concatenate([zero, rel_h], 1),
-        jnp.concatenate([zero, rel_w], 1), jnp.concatenate([rel_w, zero], 1)], 0)
-    flip_h = jnp.pad(rel_height[:54][::-1] * LOG2E, ((0, 10), (0, 32)))
-    flip_w = jnp.pad(rel_width[:54][::-1] * LOG2E, ((0, 10), (0, 32)))
-    relf = jnp.concatenate([
-        jnp.concatenate([flip_h, zero], 1), jnp.concatenate([zero, flip_h], 1),
-        jnp.concatenate([zero, flip_w], 1), jnp.concatenate([flip_w, zero], 1)], 0).T
-    relb = relb.astype(bf)
-    relf = relf.astype(bf)
-    vec = jnp.broadcast_to(jnp.stack([first_gain, first_bias, second_gain, second_bias, fc2_bias])[..., None], (5, D, 128))
-    pk = jnp.pad(pool_kernel, ((0, 0), (0, 0), (0, 32)))
-    pv = jnp.pad(jnp.concatenate([pool_gain, pool_bias], 0), ((0, 0), (0, 32)))
-
     whole = lambda v: pl.BlockSpec(v.shape, lambda i, n=v.ndim: (0,) * n)
     per = lambda: pl.BlockSpec((PAIR, D, NTOK), lambda i: (i, 0, 0))
-    consts = (wq, wqt, wpt, w1, w1t, w2, w2t, relf, relb, vec, pk, pv)
-    sums = [(208, 768), (D, 256), (208, 768), (D, 768), (256, 256), (9, 4, 8, 128), (2, 4, 8, 128), (5, D, 128), (5, D, 16)]
+    packed = [((wire.n, wire.pad, 128), bf), ((wire.n * 8, 128), f32)]
     results = pl.pallas_call(
-        kernel,
+        functools.partial(kernel, wire),
         grid=(canvases // PAIR,),
         in_specs=[pl.BlockSpec(memory_space=pltpu.SMEM), per(), per()] + [whole(v) for v in consts],
-        out_specs=[per(), per()] + [pl.BlockSpec(s, lambda i, n=len(s): (0,) * n) for s in sums],
+        out_specs=[per(), per()] + [pl.BlockSpec(s, lambda i, n=len(s): (0,) * n) for s, _ in packed],
         out_shape=[jax.ShapeDtypeStruct((canvases, D, NTOK), bf), jax.ShapeDtypeStruct((canvases, D, NTOK), f32)]
-        + [jax.ShapeDtypeStruct(s, f32) for s in sums],
+        + [jax.ShapeDtypeStruct(*s) for s in packed],
         scratch_shapes=[
+            pltpu.VMEM((FEAT, FF), f32), pltpu.VMEM((D, 256), f32), pltpu.VMEM((FEAT, FF), f32),
+            pltpu.VMEM((D, FF), f32), pltpu.VMEM((256, 256), f32), pltpu.VMEM((9, 4, 8, 128), f32),
+            pltpu.VMEM((2, 4, 8, 128), f32), pltpu.VMEM((5, D, 128), f32), pltpu.VMEM((5, D, 16), f32),
+            pltpu.VMEM((4 * D + FF, D), f32), pltpu.VMEM((wire.pad, D), f32),
             pltpu.VMEM((PAIR, 4, KVROWS, 128), f32),
             pltpu.VMEM((PAIR, 4, 272, 128), f32),
             pltpu.VMEM((PAIR, 4, NTOK, 128), f32),
@@ -455,91 +838,25 @@
         compiler_params=pltpu.CompilerParams(vmem_limit_bytes=60 * 2**20),
         name="block_step",
     )(key_crop, jnp.swapaxes(block_input, 1, 2), jnp.swapaxes(cotangent, 1, 2), *consts)
-    out, ig, gq, gp, g1, g2, grel, gpk, gpv, gln, tail = results
-    out = jnp.swapaxes(out, 1, 2)
-    ig = jnp.swapaxes(ig, 1, 2)
-
-    def unpad(v, groups):
-        lead = v.shape[:-1]
-        return v.reshape(lead + (groups, 128))[..., :HD].reshape(lead + (groups * HD,))
-
-    gq_full = unpad(gq, 6)
-    grad_qkv_weight, grad_qkv_bias = gq_full[:D], gq_full[D]
-    grad_proj_weight = unpad(gp, 2).T
-    grad_proj_bias = gp[:, HD]
-    grad_fc1_weight, grad_fc1_bias = g1[:D], g1[D]
-    grad_fc2_weight = g2.T
-    h0, h1 = grel[:HD], grel[128:128 + HD]
-    rel_pad = lambda v: jnp.pad(v.T[:54], ((0, 1), (0, 0))) * LOG2E
-    grad_rel_height = rel_pad(h0[:, 0:64] + h1[:, 64:128])
-    grad_rel_width = rel_pad(h0[:, 192:256] + h1[:, 128:192])
-    gpk = gpk.sum(2)[..., :HD]
-    grad_pool_kernel = jnp.stack([gpk[:, 0] + gpk[:, 1], gpk[:, 2] + gpk[:, 3]])
-    gpv = gpv.sum(2)[..., :HD]
-    grad_pool_gain = jnp.stack([gpv[0, 0] + gpv[0, 1], gpv[0, 2] + gpv[0, 3]])
-    grad_pool_bias = jnp.stack([gpv[1, 0] + gpv[1, 1], gpv[1, 2] + gpv[1, 3]])
-    gln = gln.sum(2) + tail.sum(2)
-    return dict(
-        out=out, ig=ig, qkv=grad_qkv_weight, proj=grad_proj_weight, fc1=grad_fc1_weight, fc2=grad_fc2_weight,
-        small=(gln[0], gln[1], grad_qkv_bias, grad_pool_kernel, grad_pool_gain, grad_pool_bias,
-               grad_rel_height, grad_rel_width, grad_proj_bias, gln[2], gln[3], grad_fc1_bias, gln[4]))
-
-
-def gather_weights(shards):
-    flat = jnp.concatenate([v.T.reshape(-1) for v in shards])
-    every = lax.all_gather(flat, ("dp", "fsdp"), axis=0, tiled=False)
-    dp, fsdp = lax.axis_size("dp"), lax.axis_size("fsdp")
-    full = []
-    start = 0
-    for v in shards:
-        rows, cols = v.shape
-        part = every[:, start:start + rows * cols].reshape(dp, fsdp, cols, rows)
-        full.append(jnp.transpose(part, (1, 3, 0, 2)).reshape(fsdp * rows, dp * cols))
-        start += rows * cols
-    return full
-
-
-def reduce_weights(grads, shards):
-    dp, fsdp = lax.axis_size("dp"), lax.axis_size("fsdp")
-    parts = []
-    for grad, v in zip(grads, shards):
-        rows, cols = v.shape
-        part = jnp.transpose(grad.astype(bf).reshape(fsdp, rows, dp, cols), (2, 0, 3, 1))
-        parts.append(part.reshape(dp * fsdp, cols * rows))
-    flat = jnp.concatenate(parts, 1)
-    mine = lax.psum_scatter(flat, ("dp", "fsdp"), scatter_dimension=0, tiled=False).astype(f32)
-    owned = []
-    start = 0
-    for v in shards:
-        rows, cols = v.shape
-        owned.append(mine[start:start + rows * cols].reshape(cols, rows).T)
-        start += rows * cols
-    return owned
+    out, ig, grads, small = results
+    return jnp.swapaxes(out, 1, 2), jnp.swapaxes(ig, 1, 2), grads, small
 
 
 def local(
-    block_input, token_crop, key_crop, first_gain, first_bias, qkv_weight, qkv_bias, pool_kernel, pool_gain,
+    wire, block_input, token_crop, key_crop, first_gain, first_bias, qkv_weight, qkv_bias, pool_kernel, pool_gain,
     pool_bias, rel_height, rel_width, proj_weight, proj_bias, second_gain, second_bias, fc1_weight, fc1_bias,
     fc2_weight, fc2_bias, cotangent,
 ):
-    shards = (qkv_weight, proj_weight, fc1_weight, fc2_weight)
-    qkv_full, proj_full, fc1_full, fc2_full = gather_weights(shards)
-    r = compute(
-        block_input, key_crop, first_gain, first_bias, qkv_full, qkv_bias, pool_kernel, pool_gain, pool_bias,
-        rel_height, rel_width, proj_full, proj_bias, second_gain, second_bias, fc1_full, fc1_bias, fc2_full,
-        fc2_bias, cotangent)
-    owned = reduce_weights((r["qkv"], r["proj"], r["fc1"], r["fc2"]), shards)
-    small = r["small"]
-    flat = jnp.concatenate([v.reshape(-1) for v in small])
-    flat = lax.psum(flat, ("dp", "fsdp"))
-    summed = []
-    start = 0
-    for v in small:
-        summed.append(flat[start:start + v.size].reshape(v.shape))
-        start += v.size
-    return (
-        r["out"], r["ig"], summed[0], summed[1], owned[0], summed[2], summed[3], summed[4], summed[5], summed[6],
-        summed[7], owned[1], summed[8], summed[9], summed[10], owned[2], summed[11], owned[3], summed[12])
+    consts = gather(
+        wire, (qkv_weight, proj_weight, fc1_weight, fc2_weight),
+        (qkv_bias, proj_bias, fc1_bias, first_gain, first_bias, second_gain, second_bias, fc2_bias,
+         jnp.transpose(pool_kernel, (1, 0, 2)), pool_gain, pool_bias, rel_height, rel_width))
+    out, ig, grads, small = compute(wire, block_input, key_crop, cotangent, consts)
+    res, rows = reduce(wire, grads, small.reshape(wire.n, 8, 128))
+    (qkv, proj, fc1, fc2, qkv_b, proj_b, fc1_b, gain1, shift1, gain2, shift2, fc2_b, taps, pool_g, pool_s, rel_h,
+     rel_w) = finish(wire, res, rows)
+    return (out, ig, gain1, shift1, qkv.T, qkv_b, jnp.transpose(taps, (1, 0, 2)), pool_g, pool_s, rel_h, rel_w,
+            proj.T, proj_b, gain2, shift2, fc1.T, fc1_b, fc2.T, fc2_b)
 
 
 def solution(mesh):
@@ -547,8 +864,9 @@
     ids = P(("dp", "fsdp"), None)
     block = P("fsdp", "dp")
     one = P()
+    wire = Wire(mesh.shape["dp"], mesh.shape["fsdp"])
     return jax.shard_map(
-        local,
+        functools.partial(local, wire),
         mesh=mesh,
         in_specs=(rows, ids, ids, one, one, block, one, one, one, one, one, one, block, one, one, one, block, one,
                   block, one, rows),

time: 374 us -> 186 us (0.50)
  blocking collectives: 117 us -> 0 us
  waiting for transfers between devices: 79.4 us -> 0 us
  Pallas kernels: 127 us -> 186 us
  local copies, waits for them, and re-layouts: 25.8 us -> 0 us
  between operations: 14.9 us -> 0.68 us
  other arithmetic: 8.9 us -> 0 us
    all_gather x1 -> x0, blocking collectives: 79.5 us -> none  [gather_weights(): every = lax.all_gather(flat, ('dp', 'fsdp'), axis=0, tiled=False)]
    unnamed x2 -> x0, waiting for transfers between devices: 79.4 us -> none
    pallas_call x1 -> x4, Pallas kernels: 127 us -> 186 us  [the longest x1 129 us: compute(): pl.pallas_call(functools.partial(kernel, wire), grid=(canvases // PAIR,),...]
    psum x1 -> x0, blocking collectives: 37.7 us -> none  [local(): flat = lax.psum(flat, ('dp', 'fsdp'))]
    reshape x33 -> x0, local copies, waits for them, and re-layouts: 11.4 us -> none  [the longest x4 3.08 us: gather_weights(): flat = jnp.concatenate([v.T.reshape(-1) for v in shards])]
    slice x22 -> x0, local copies, waits for them, and re-layouts: 6.75 us -> none  [the longest x6 2.14 us: reduce_weights(): owned.append(mine[start:start + rows * cols].reshape(cols, rows).T)]
  transfers between devices with their start and end apart: 1 -> 0, of which waited for: 1 -> 0; matrix products, arithmetic and copies ran while one was open for 2% -> 0% of each run, Pallas kernels for 0% -> 0%
where the time goes in v2:
time: 186 us
  Pallas kernels  186 us (100%)
    pallas_call x1, Pallas kernels, compute(): pl.pallas_call(functools.partial(kernel, wire), grid=(canvases // PAIR,),...  129 us
    pallas_call x3, Pallas kernels, staged_call(): pl.pallas_call(functools.partial(staged, body, ins, shapes), in_specs=[hb...  56.3 us

profile of v2, /device:TPU:0, one launch (start us, length us, event | category | flops | bytes accessed | tf_op | source)
XLA Modules:
  0.0 186.2 jit_solution(17529561955447918068)
XLA Ops:
  0.7 26.0 %gather_weights.1 = (bf16[208,768]{1,0:T(8,128)(2,1)}, bf16[192,256]{1,0:T(8,128)(2,1)}, bf16[208,768]{1,0:T(8,128)(2,1)}, bf16[192,768]{1,0:T(8,128)(2,1)}, bf1...) custom-call(bf16[36,96]{1,0:T(8,128)(2,1)} %bitcast.22, ...), custom_call_target="tpu_custom_call" | custom-call | tf_op jit(solution)/shard_map/gather_weights/pallas_call | solution.py:631
  26.7 129.3 %block_step.1 = (bf16[16,192,784]{2,1,0:T(8,128)(2,1)}, f32[16,192,784]{2,1,0:T(8,128)}, bf16[32,144,128]{2,1,0:T(8,128)(2,1)}, f32[256,128]{1,0:T(8,128)}) custom-call(s32[16,196]{1,0:T(8,128)} %kc_ref.1, bf16[16,192,784]{2,1,0:T(8,128)(2,1)} %bitcast.16, bf16[16,192,784]{2,1,0:T(8,128)(2,1)} %bitcast.17, bf16[208,768]{1,0:T(8,128)(2,1)} %get-tuple-element.51.wq_ref, ...), custom_call_target="tpu_custom_call" | custom-call | tf_op jit(solution)/shard_map/block_step/pallas_call | solution.py:819
  156.0 28.4 %reduce_gradients.1 = (f32[144,128]{1,0:T(8,128)}, f32[32,8,128]{2,1,0:T(8,128)}) custom-call(bf16[32,144,128]{2,1,0:T(8,128)(2,1)} %get-tuple-element.62.refs_0_, f32[32,8,128]{2,1,0:T(8,128)} %bitcast.18), custom_call_target="tpu_custom_call" | custom-call | tf_op jit(solution)/shard_map/reduce_gradients/pallas_call | solution.py:631
  184.4 1.8 split_gradients.1

commit v3 on v2

--- a/solution.py
+++ b/solution.py
@@ -26,8 +26,11 @@
 KVROWS = BASE + NTOK + 24
 bf = jnp.bfloat16
 PAIR = 2
-SKEW = 3
+SKEW = 8
+EVERY = 1
 FEAT = 208
+MAIN = 768
+REST = 16
 f32 = jnp.float32
 
 
@@ -62,9 +65,9 @@
     return total
 
 
-def add_lanes(ref, tail, n, v):
-    ref[n] += fold_lanes(v)
-    tail[n] += v[:, 768:784]
+def add_lanes(ref, tail, v):
+    ref[...] += fold_lanes(v)
+    tail[...] += v[:, 768:784]
 
 
 def with_ones(v):
@@ -137,13 +140,14 @@
 
 
 def kernel(
-    wire, kc_ref, x_ref, g_ref, wq_ref, wpt_ref, w1_ref, w2t_ref,
+    wire, steps_of, kc_ref, x_ref, g_ref, wq_ref, wpt_ref, w1_ref, w2t_ref, wqt_ref, wp_ref, w1t_ref, w2_ref,
     relf_ref, relb_ref, vec_ref, pk_ref, pv_ref,
     out_ref, ig_ref, wire_ref, small_ref,
     gq_ref, gp_ref, g1_ref, g2_ref, grel_ref, gpk_ref, gpv_ref, gln_ref, tail_ref, table, piece,
-    kvs, gps, gkvs, kf, kb, vx,
+    kvs, gps, gkvs, kf, kb, vx, *spare,
 ):
     step = pl.program_id(0)
+    spare = [(spare[2 * k], spare[2 * k + 1]) for k in range(4)]
 
     @pl.when(step == 0)
     def _():
@@ -168,15 +172,16 @@
             vx[c, h, :, :128] = jnp.zeros((256, 128), bf)
             vx[c, h, :, 128:] = jnp.ones((256, 128), bf)
 
+    pairs = Pairs(step, dict(gq=gq_ref, gp=gp_ref, g1=g1_ref, g2=g2_ref), dict(zip(("gq", "gp", "g1", "g2"), spare)))
+    later = pairs.later
     steps = [
         canvas(
-            step * PAIR + c, c, kc_ref, x_ref, g_ref, wq_ref, wpt_ref, w1_ref, w2t_ref,
+            pairs, step * PAIR + c, c, kc_ref, x_ref, g_ref, wq_ref, wpt_ref, w1_ref, w2t_ref, wqt_ref, wp_ref, w1t_ref, w2_ref,
             relf_ref, relb_ref, vec_ref, pk_ref, pv_ref,
             out_ref, ig_ref, gq_ref, gp_ref, g1_ref, g2_ref, grel_ref, gpk_ref, gpv_ref, gln_ref, tail_ref,
             kvs.at[c], gps.at[c], gkvs.at[c], kf.at[c], kb.at[c], vx.at[c])
         for c in range(PAIR)]
     live = list(steps)
-    started = 0
     tick = 0
     while live:
         for c, one in enumerate(steps):
@@ -185,17 +190,35 @@
                     next(one)
                 except StopIteration:
                     live.remove(one)
+                if later and tick % EVERY == 0:
+                    later.pop(0)()
         tick += 1
+    while later:
+        later.pop(0)()
 
     @pl.when(step == pl.num_programs(0) - 1)
     def _():
-        pack(wire, wire_ref, small_ref, gq_ref, gp_ref, g1_ref, g2_ref, grel_ref, gpk_ref, gpv_ref, gln_ref,
+        pairs.finish(steps_of)
+        pack(wire, wq_ref, w1_ref, vec_ref, wire_ref, small_ref, gq_ref, gp_ref, g1_ref, g2_ref, grel_ref, gpk_ref, gpv_ref, gln_ref,
              tail_ref, table, piece)
 
 
-def pack(wire, wire_ref, small_ref, gq_ref, gp_ref, g1_ref, g2_ref, grel_ref, gpk_ref, gpv_ref, gln_ref, tail_ref,
+def pack(wire, wq_ref, w1_ref, vec_ref, wire_ref, small_ref, gq_ref, gp_ref, g1_ref, g2_ref, grel_ref, gpk_ref, gpv_ref, gln_ref, tail_ref,
          table, piece):
     wide = wire.width
+    gain1, shift1, gain2, shift2 = [vec_ref[k] for k in range(4)]
+    norm_rows = []
+    for ref, w_ref, gain, shift in ((gq_ref, wq_ref, gain1, shift1), (g1_ref, w1_ref, gain2, shift2)):
+        by_gain, by_shift = 0.0, 0.0
+        for g in range(6):
+            cols = slice(128 * g, 128 * g + 128)
+            w = w_ref[:D, cols].astype(f32)
+            sums = ref[D:D + 1, cols]
+            by_gain = by_gain + w * ref[:D, cols]
+            by_shift = by_shift + w * sums
+            ref[:D, cols] = gain * ref[:D, cols] + shift * sums
+        for v in (by_gain, by_shift):
+            norm_rows.append(jnp.sum(jnp.transpose(v / gain), 0, keepdims=True))
     for g in range(6):
         table[HD * g:HD * g + HD, :] = jnp.transpose(gq_ref[:D, 128 * g:128 * g + 128])[:HD]
     table[3 * D:4 * D, :] = jnp.concatenate([gp_ref[:, 0:HD], gp_ref[:, 128:128 + HD]], 1)
@@ -204,7 +227,7 @@
     for d in range(wire.dp):
         for first, count, at in wire.starts(d):
             piece[first:first + count, :] = table[at:at + count, :]
-        low = g2_ref[wire.low * d:wire.low * (d + 1), :]
+        low = g2_ref[wire.low * d:wire.low * (d + 1), :] * 0.5
         for f in range(wire.fsdp):
             for q in range(wire.parts):
                 first = wire.top + q * wire.low
@@ -212,8 +235,7 @@
                 piece[first:first + wire.low, f * wide:(f + 1) * wide] = low[:, at:at + wide]
         for f in range(wire.fsdp):
             part = piece[:, f * wide:(f + 1) * wide]
-            part = jnp.concatenate([part, jnp.zeros((wire.pad, 128 - wide), f32)], 1)
-            wire_ref[wire.slot(d, f)] = part.astype(bf)
+            wire_ref[wire.slot(d, f)] = wire.fold(part[:wire.top], part[wire.top:wire.used]).astype(bf)
     small_ref[...] = jnp.zeros_like(small_ref)
     turned = jnp.transpose(grel_ref[...]) * LOG2E
     small_ref[0:64] = turned[0:64, 0:128] + turned[64:128, 128:256]
@@ -228,18 +250,52 @@
     for g in range(6):
         small_ref[152 + g:153 + g] = gq_ref[D:D + 1, 128 * g:128 * g + 128]
         small_ref[158 + g:159 + g] = g1_ref[D:D + 1, 128 * g:128 * g + 128]
-    rows = []
-    for k in range(5):
-        rows.append(jnp.sum(jnp.transpose(gln_ref[k]), 0, keepdims=True)
-                    + jnp.sum(jnp.transpose(tail_ref[k]), 0, keepdims=True))
+    rows = norm_rows + [jnp.sum(jnp.transpose(gln_ref[...]), 0, keepdims=True)
+                        + jnp.sum(jnp.transpose(tail_ref[...]), 0, keepdims=True)]
     rows.append(jnp.transpose(gp_ref[:, 0:128])[HD:HD + 1])
     for k, v in enumerate(rows):
         small_ref[164 + 2 * k:165 + 2 * k] = v[:, 0:128]
         small_ref[165 + 2 * k:166 + 2 * k] = jnp.concatenate([v[:, 128:D], jnp.zeros((1, 256 - D), f32)], 1)
 
 
+def features(v, w):
+    return jnp.transpose(dot(v, w)[:, :D])
+
+
+def add_dot(ref, cols, left, right):
+    ref[:, cols] += dot(left, right)
+
+
+class Pairs:
+    def __init__(self, step, totals, spare):
+        self.step, self.totals, self.spare = step, totals, spare
+        self.later, self.held = [], {}
+
+    def add(self, name, slot, left, right):
+        self.held.setdefault(name, []).append((slot, left, right))
+        if len(self.held[name]) < PAIR:
+            return
+        both = sorted(self.held.pop(name), key=lambda v: v[0])
+        total = self.totals[name]
+        left = jnp.concatenate([v[1][:, :MAIN] for v in both], 1)
+        right = jnp.concatenate([v[2][:MAIN] for v in both], 0)
+        for n in range(0, right.shape[1], 256):
+            cols = slice(n, n + 256)
+            self.later.append(functools.partial(add_dot, total, cols, left, right[:, cols]))
+        keep_left, keep_right = self.spare[name]
+        keep_left[self.step] = jnp.concatenate([v[1][:, MAIN:] for v in both], 1)
+        rows = PAIR * REST
+        keep_right[pl.ds(pl.multiple_of(self.step * rows, rows), rows), :] = jnp.concatenate([v[2][MAIN:] for v in both], 0)
+
+    def finish(self, steps):
+        for name, total in self.totals.items():
+            keep_left, keep_right = self.spare[name]
+            left = jnp.concatenate([keep_left[k] for k in range(steps)], 1)
+            total[...] += dot(left, keep_right[...])
+
+
 def canvas(
-    item, slot, kc_ref, x_ref, g_ref, wq_ref, wpt_ref, w1_ref, w2t_ref,
+    pairs, item, slot, kc_ref, x_ref, g_ref, wq_ref, wpt_ref, w1_ref, w2t_ref, wqt_ref, wp_ref, w1t_ref, w2_ref,
     relf_ref, relb_ref, vec_ref, pk_ref, pv_ref,
     out_ref, ig_ref, gq_ref, gp_ref, g1_ref, g2_ref, grel_ref, gpk_ref, gpv_ref, gln_ref, tail_ref,
     kvs, gps, gkvs, kf, kb, vx,
@@ -248,11 +304,11 @@
     mask96 = (lane128 < HD).astype(f32)
     lowhalf = iota((NTOK, 128), 1) < 64
 
-    gain1, shift1, gain2, shift2, fc2_bias = [lanes(vec_ref[n]) for n in range(5)]
+    fc2_bias = lanes(vec_ref[4])
 
     x = x_ref[slot].astype(f32)
     u1, r1 = norm_cols(x)
-    nb = with_ones((u1 * gain1 + shift1).astype(bf))
+    nb = with_ones(u1.astype(bf))
     qb = dot_tn(nb, wq_ref[:, :256]).astype(bf)
     for n in range(4):
         kvs[n, BASE:BASE + NTOK, :] = dot_tn(nb, wq_ref[:, 256 + 128 * n:384 + 128 * n])
@@ -262,24 +318,26 @@
 
     def tap(n, x_row, b):
         v = kvs.at[n][pl.ds(BASE + SIDE * x_row + b - 1, 16, stride=2), :]
-        return v * notfirst if b == 0 else v
+        return v
 
     u_pool, r_pool = [], []
     for n in range(4):
         w = n // 2
+        taps = [pk_ref[w, k:k + 1] for k in range(9)]
+        taps = [v * notfirst if k % 3 == 0 else v for k, v in enumerate(taps)]
         rows = []
         for i in range(KS):
             acc = None
             for a in range(3):
                 for b in range(3):
-                    t = tap(n, 2 * i + a - 1, b) * pk_ref[w, 3 * a + b:3 * a + b + 1]
+                    t = tap(n, 2 * i + a - 1, b) * taps[3 * a + b]
                     acc = t if acc is None else acc + t
             rows.append(acc)
-        yield
         u, r = norm_parts(jnp.concatenate(rows, 0), mask96, HD)
         u_pool.append(u)
         r_pool.append(r)
         val = u * pv_ref[w:w + 1] + pv_ref[2 + w:3 + w]
+        yield
         h = n % 2
         if w == 0:
             val = val * (SCALE * LOG2E)
@@ -289,7 +347,6 @@
         else:
             vx[h, 0:224, :128] = val.astype(bf)
 
-    yield
     row_cut = 0
     col_cut = 0
     for n in range(KS):
@@ -304,15 +361,18 @@
     y56 = jnp.where(y56 >= SIDE, y56 - SIDE, y56)
     col_bias = jnp.where((y56 >= col_cut) != col_side, FILL, 0.0)
 
+    yield
     a_h = dot(qb, relf_ref[:, :128])
     a_w = dot(qb, relf_ref[:, 128:])
     pieces_h = roll_x(a_h)
+    yield
     pieces_w = roll_y(a_w)
     done_h, done_w = [], []
     for p in range(KS):
         row_bias = jnp.where(2 * p >= row_cut, rows_after, rows_before)
         done_h.append(jnp.concatenate(pieces_h[3 * p:3 * p + 3], 0) + row_bias)
         done_w.append(jnp.concatenate(pieces_w[3 * p:3 * p + 3], 0) + col_bias)
+    yield
     t_h = jnp.concatenate(done_h, 0)
     t_w = jnp.concatenate(done_w, 0)
     rel = (jnp.where(lowhalf, t_h, t_w).astype(bf), jnp.where(lowhalf, t_w, t_h).astype(bf))
@@ -327,51 +387,57 @@
         o = dot(e, vx[h])
         rinv = 1.0 / o[:, 128:]
         eb.append(e)
-        inv.append(rinv)
+        inv.append(rinv * LN2)
         mixed.append(o[:, :128] * rinv)
+    yield
     ab = (jnp.concatenate(mixed, 1) + qb.astype(f32)).astype(bf)
 
     yield
-    middle = x + dot_nt(wpt_ref[...], ab)
+    middle = x + features(ab, wp_ref[...])
     u2, r2 = norm_cols(middle)
-    n2b = with_ones((u2 * gain2 + shift2).astype(bf))
+    n2b = with_ones(u2.astype(bf))
     gb = g_ref[slot]
+    yield
     act, gh = [], []
     for n in range(3):
         cols = slice(256 * n, 256 * n + 256)
         hid = dot_tn(n2b, w1_ref[:, cols])
-        phi = 0.5 * lax.erf(hid * 0.7071067811865476) + 0.5
-        slope = phi + hid * jnp.exp2(hid * hid * (-0.5 * LOG2E)) * 0.3989422804014327
+        gact = dot_tn(gb, w2t_ref[:, cols])
         yield
+        z = hid * 0.7071067811865476
+        phi = 1.0 + lax.erf(z)
+        slope = phi + z * (jnp.exp2(z * z * (-LOG2E)) * 1.1283791670955126)
         act.append((hid * phi).astype(bf))
-        gh.append((dot_tn(gb, w2t_ref[:, cols]) * slope).astype(bf))
-    yield
+        gh.append((gact * slope).astype(bf))
+        yield
     act = jnp.concatenate(act, 1)
     gh = jnp.concatenate(gh, 1)
-    out = middle + fc2_bias + dot_nt(w2t_ref[...], act)
+    out = middle + fc2_bias + features(act, w2_ref[...])
     out_ref[slot] = out.astype(bf)
-    g2_ref[...] += dot(gb, act)
-    g1_ref[...] += dot(n2b, gh)
+    pairs.add("g2", slot, gb, act)
+    pairs.add("g1", slot, n2b, gh)
     yield
     g = gb.astype(f32)
-    add_lanes(gln_ref, tail_ref, 4, g)
-    e2 = dot_nt(w1_ref[:D], gh)
-    add_lanes(gln_ref, tail_ref, 2, e2 * u2)
-    add_lanes(gln_ref, tail_ref, 3, e2)
-    gm = g + norm_cols_back(e2 * gain2, u2, r2)
+    add_lanes(gln_ref, tail_ref, g)
+    ge = features(gh, w1t_ref[...])
+    yield
+    gm = g + norm_cols_back(ge, u2, r2)
     grb = gm.astype(bf)
-    gp_ref[...] += dot(grb, ab)
-    yield
-    gatt = dot_tn(grb, wpt_ref[...]).astype(bf).astype(f32)
+    pairs.add("gp", slot, grb, ab)
+    yield
+    yield
+    gatt = dot_tn(grb, wpt_ref[...])
     gr, gcont = [], []
     g2bs, dss = [], []
     for h in range(HEADS):
         ga = gatt[:, 128 * h:128 * h + 128]
-        g2b = (ga * (inv[h] * LN2)).astype(bf)
-        dd = jnp.sum(g2b.astype(f32) * mixed[h], -1, keepdims=True)
+        ga = ga * inv[h]
+        g2b = ga.astype(bf)
+        dd = jnp.sum(ga * mixed[h], -1, keepdims=True)
         yield
         gpr = dot_nt(g2b, vx[h, :, :128])
-        ds = (eb[h].astype(f32) * (gpr - dd)).astype(bf)
+        ds = eb[h] * (gpr - dd).astype(bf)
+        yield
         back = dot(ds, kb[h])
         gcont.append(back[:, :128])
         gr.append(back[:, 128:])
@@ -379,6 +445,7 @@
         g2bs.append(g2b)
     yield
     b_h = jnp.concatenate(roll_x(jnp.where(lowhalf, gr[0], gr[1])), 0)
+    yield
     b_w = jnp.concatenate(roll_y(jnp.where(lowhalf, gr[1], gr[0])), 0)
     gab = jnp.concatenate([b_h, b_w], 1).astype(bf)
     gq = jnp.concatenate(gcont, 1) + dot(gab, relb_ref[...]) + gatt
@@ -397,19 +464,21 @@
         gpv_ref[1, n] += fold(e)
         gps[n, 0:224, :] = norm_back(e * pv_ref[w:w + 1], u_pool[n], r_pool[n], HD)
 
-    yield
     for n in range(4):
         w = n // 2
         for a in range(3):
+            yield
             for b in range(3):
                 acc = None
                 for i in range(KS):
                     t = gps[n, 16 * i:16 * i + 16, :] * tap(n, 2 * i + a - 1, b)
                     acc = t if acc is None else acc + t
+                if b == 0:
+                    acc = acc * notfirst
                 gpk_ref[3 * a + b, n] += acc[0:8] + acc[8:16]
 
+
         yield
-
         def wk(a, b):
             return pk_ref[w, 3 * a + b:3 * a + b + 1]
 
@@ -432,12 +501,10 @@
 
     yield
     gpk = jnp.concatenate([gq.astype(bf)] + [gkvs[n].astype(bf) for n in range(4)], 1)
-    gq_ref[...] += dot(nb, gpk)
-    e1 = dot_nt(wq_ref[:D], gpk)
-    yield
-    add_lanes(gln_ref, tail_ref, 0, e1 * u1)
-    add_lanes(gln_ref, tail_ref, 1, e1)
-    ig_ref[slot] = gm + norm_cols_back(e1 * gain1, u1, r1)
+    pairs.add("gq", slot, nb, gpk)
+    ge = features(gpk, wqt_ref[...])
+    yield
+    ig_ref[slot] = gm + norm_cols_back(ge, u1, r1)
 
 
 MESH = pl.DeviceIdType.MESH
@@ -447,6 +514,7 @@
     def __init__(self, dp, fsdp):
         self.dp, self.fsdp, self.n = dp, fsdp, dp * fsdp
         self.chips = self.n // 2
+        self.line, self.plane = dp // 4, 2 * fsdp
         self.rows = (3 * D // dp, D // dp, FF // dp)
         self.top = sum(self.rows)
         self.low = D // dp
@@ -454,43 +522,73 @@
         self.parts = FF // fsdp // self.width
         self.used = self.top + self.parts * self.low
         self.pad = -(-self.used // 16) * 16
+        self.lows = self.parts * self.low
+        self.dense = self.width == 96 and self.top == 2 * self.lows and self.lows % 48 == 0
+        self.full = self.top + self.lows // 3 if self.dense else self.pad
+
+    def fold(self, top, low, *more):
+        rows = self.lows
+        if self.dense:
+            third = rows // 3
+            parts = [
+                jnp.concatenate([top[:rows], low[:, 0:32]], 1),
+                jnp.concatenate([top[rows:], low[:, 32:64]], 1),
+                jnp.concatenate([low[k * third:(k + 1) * third, 64:96] for k in range(3)]
+                                + [jnp.zeros((third, 32), top.dtype)], 1)]
+        else:
+            parts = [jnp.concatenate([v, jnp.zeros((v.shape[0], 128 - self.width), top.dtype)], 1) for v in (top, low)]
+            if self.pad > self.used:
+                parts.append(jnp.zeros((self.pad - self.used, 128), top.dtype))
+        return jnp.concatenate(parts + list(more), 0)
+
+    def unfold(self, block):
+        rows, wide = self.lows, self.width
+        if not self.dense:
+            return block[:self.top, :wide], block[self.top:self.used, :wide]
+        third = rows // 3
+        last = jnp.concatenate([block[self.top:self.top + third, 32 * k:32 * k + 32] for k in range(3)], 0)
+        low = jnp.concatenate([block[:rows, 96:128], block[rows:2 * rows, 96:128], last], 1)
+        return block[:self.top, :wide], low
 
     def starts(self, d):
         a, b, c = self.rows
         return ((0, a, a * d), (a, b, 3 * D + b * d), (a + b, c, 4 * D + c * d))
 
     def slot(self, d, f):
-        return (d % 2) * self.chips + (d // 2) * self.fsdp + f
+        return (d % 2) * self.chips + ((d // 2) % 2 * self.fsdp + f) * self.line + d // 4
 
     def place(self):
         d, f = lax.axis_index("dp"), lax.axis_index("fsdp")
-        core = lax.rem(d, 2)
-        return core, (d // 2) * self.fsdp + f
-
-    def device(self, core, chip):
-        return (2 * (chip // self.fsdp) + core, lax.rem(chip, self.fsdp))
+        return lax.rem(d, 2), lax.rem(d // 2, 2) * self.fsdp + f, d // 4
+
+    def peer(self, slot):
+        chip = lax.rem(slot, self.chips)
+        return self.device(slot // self.chips, chip // self.line, lax.rem(chip, self.line))
+
+    def device(self, core, q, z):
+        return (4 * z + 2 * (q // self.fsdp) + core, lax.rem(q, self.fsdp))
+
+
+def greet_near(wire):
+    line, plane = wire.line, wire.plane
+    core, q, z = wire.place()
+    friends = [wire.device(1 - core, q, z)]
+    friends += [wire.device(core, q, lax.rem(z + k, line)) for k in range(1, line)]
+    friends += [wire.device(core, lax.rem(q + j, plane), z) for j in range(1, plane)]
+    for friend in friends:
+        pl.semaphore_signal(pltpu.get_barrier_semaphore(), inc=1, device_id=friend, device_id_type=MESH)
 
 
 def gather_kernel(
     wire, qkv, proj, fc1, fc2, qkv_bias, proj_bias, fc1_bias, gain1, shift1, gain2, shift2, fc2_bias,
     pool_kernel, pool_gain, pool_bias, rel_h, rel_w,
-    wq_ref, wpt_ref, w1_ref, w2t_ref, relf_ref, relb_ref, vec_ref, pk_ref, pv_ref,
-    buf, mine, tmp, table, low_table, send, forward, recv,
+    wq_ref, wpt_ref, w1_ref, w2t_ref, wqt_ref, wp_ref, w1t_ref, w2_ref, relf_ref, relb_ref, vec_ref, pk_ref, pv_ref,
+    buf, tmp, table, low_table, line_send, plane_send, core_send, recv,
 ):
-    n, nc = wire.n, wire.chips
-    core, chip = wire.place()
+    nc, line, plane = wire.chips, wire.line, wire.plane
+    core, q, z = wire.place()
     other = 1 - core
-    partner = wire.device(other, chip)
-    me = core * nc + chip
-    barrier = pltpu.get_barrier_semaphore()
-    pl.semaphore_signal(barrier, inc=1, device_id=partner, device_id_type=MESH)
-
-    def greet(k, c):
-        pl.semaphore_signal(barrier, inc=1, device_id=wire.device(core, lax.rem(chip + k, nc)), device_id_type=MESH)
-        return c
-
-    lax.fori_loop(1, nc, greet, 0)
-
+    me = core * nc + q * line + z
     wide = wire.width
     a, b, c = wire.rows
     tmp[...] = jnp.zeros_like(tmp)
@@ -498,28 +596,34 @@
     tmp[a:a + b, :wide] = proj[...].astype(f32)
     tmp[a + b:wire.top, :wide] = fc1[...].astype(f32)
     below = fc2[...].astype(f32)
-    for q in range(wire.parts):
-        first = wire.top + q * wire.low
-        tmp[first:first + wire.low, :wide] = below[:, q * wide:(q + 1) * wide]
-    mine[...] = tmp[:, :128].astype(bf)
-    pl.semaphore_wait(barrier, nc)
-
-    def to_partner(src, slot, k):
+    for p in range(wire.parts):
+        first = wire.top + p * wire.low
+        tmp[first:first + wire.low, :wide] = below[:, p * wide:(p + 1) * wide]
+    buf[pl.ds(me, 1)] = tmp[:, :128].astype(bf)[None]
+    pl.semaphore_wait(pltpu.get_barrier_semaphore(), line + plane - 1)
+
+    def held(k, j):
+        return core * nc + lax.rem(q + j, plane) * line + lax.rem(z + k, line)
+
+    def copy(slot, sem, device):
         return pltpu.make_async_remote_copy(
-            src_ref=src, dst_ref=buf.at[slot], send_sem=forward.at[k], recv_sem=recv.at[slot],
-            device_id=partner, device_id_type=MESH)
-
-    def to_chip(k):
-        return pltpu.make_async_remote_copy(
-            src_ref=mine, dst_ref=buf.at[me], send_sem=send.at[k], recv_sem=recv.at[me],
-            device_id=wire.device(core, lax.rem(chip + k, nc)), device_id_type=MESH)
-
-    def start(k, c):
-        to_chip(nc - k).start()
-        return c
-
-    lax.fori_loop(1, nc, start, 0)
-    to_partner(mine, me, 0).start()
+            src_ref=buf.at[slot], dst_ref=buf.at[slot], send_sem=sem, recv_sem=recv.at[slot],
+            device_id=device, device_id_type=MESH)
+
+    def to_line(k):
+        return copy(me, line_send.at[k], wire.device(core, q, lax.rem(z + k, line)))
+
+    def to_plane(k, j):
+        return copy(held(k, 0), plane_send.at[k * plane + j], wire.device(core, lax.rem(q + j, plane), z))
+
+    def to_core(k, j):
+        return copy(held(k, j), core_send.at[k * plane + j], wire.device(other, q, z))
+
+    for k in range(1, line):
+        to_line(k).start()
+    for j in range(1, plane):
+        to_plane(0, j).start()
+    to_core(0, 0).start()
 
     def row(ref):
         return ref[...].reshape(1, ref.shape[0])
@@ -548,22 +652,17 @@
     four = jnp.concatenate([pool_gain[...], pool_bias[...]], 0)
     pv_ref[...] = jnp.concatenate([four, jnp.zeros((4, 128 - HD), f32)], 1)
 
-    def relay(k, c):
-        slot = core * nc + lax.rem(chip + k, nc)
-        pltpu.make_async_remote_copy(
-            src_ref=mine, dst_ref=buf.at[slot], send_sem=send.at[0], recv_sem=recv.at[slot],
-            device_id=partner, device_id_type=MESH).wait_recv()
-        to_partner(buf.at[slot], slot, k).start()
-        return c
-
-    lax.fori_loop(1, nc, relay, 0)
-
-    def arrive(k, c):
-        to_partner(mine, other * nc + k, 0).wait_recv()
-        return c
-
-    lax.fori_loop(0, nc, arrive, 0)
-    buf[pl.ds(me, 1)] = mine[...][None]
+    for k in range(1, line):
+        to_core(k, 0).wait_recv()
+        for j in range(1, plane):
+            to_plane(k, j).start()
+        to_core(k, 0).start()
+    for k in range(line):
+        for j in range(1, plane):
+            to_core(k, j).wait_recv()
+            to_core(k, j).start()
+    for c in range(nc):
+        copy(other * nc + c, core_send.at[0], wire.device(other, q, z)).wait_recv()
 
     for d in range(wire.dp):
         blocks = [buf[wire.slot(d, f)].astype(f32) for f in range(wire.fsdp)]
@@ -582,10 +681,15 @@
 
     qb = row(qkv_bias)
     for g in range(6):
-        block = jnp.concatenate([jnp.transpose(table[HD * g:HD * g + HD, :]), two(qb[:, HD * g:HD * g + HD])], 0)
+        w = jnp.transpose(table[HD * g:HD * g + HD, :])
+        bias = qb[:, HD * g:HD * g + HD] + jnp.sum(w * vec_ref[1][:, :HD], 0, keepdims=True)
+        block = jnp.concatenate([w * vec_ref[0][:, :HD], two(bias)], 0)
         spare = (iota((FEAT, 128 - HD), 0) == D) & (iota((FEAT, 128 - HD), 1) == 0) & (g < 2)
         block = jnp.concatenate([block, jnp.where(spare, 1.0, 0.0)], 1)
         wq_ref[:, 128 * g:128 * g + 128] = block.astype(bf)
+        flat = table[HD * g:HD * g + HD, :] * row(gain1)
+        flat = jnp.concatenate([flat, jnp.zeros((128 - HD, D), f32)], 0)
+        wqt_ref[128 * g:128 * g + 128, :] = widen(flat).astype(bf)
     cols = []
     pb = row(proj_bias)
     hi = pb.astype(bf).astype(f32)
@@ -593,24 +697,33 @@
         col = jnp.transpose(jnp.broadcast_to(extra, (128, D)))[:, :128 - HD]
         col = jnp.where(iota((D, 128 - HD), 1) == 0, col, 0.0)
         cols += [table[3 * D:4 * D, HD * g:HD * g + HD], col]
-    wpt_ref[...] = jnp.concatenate(cols, 1).astype(bf)
-    w1_ref[...] = jnp.concatenate([jnp.transpose(table[4 * D:4 * D + FF, :]), two(row(fc1_bias))], 0).astype(bf)
-    w2t_ref[...] = low_table[...].astype(bf)
-
-    def finish(k, c):
-        to_chip(k).wait_send()
-        to_partner(mine, me, k).wait_send()
-        return c
-
-    lax.fori_loop(1, nc, finish, 0)
-    to_partner(mine, me, 0).wait_send()
-
-
-def staged(body, ins, outs, *refs):
+    wpt = jnp.concatenate(cols, 1)
+    wpt_ref[...] = wpt.astype(bf)
+    wp_ref[...] = widen(jnp.transpose(wpt)).astype(bf)
+    w1t_ref[...] = widen(table[4 * D:4 * D + FF, :] * row(gain2)).astype(bf)
+    w2_ref[...] = widen(jnp.transpose(low_table[...]) * 0.5).astype(bf)
+    fb = row(fc1_bias)
+    for g in range(6):
+        w = jnp.transpose(table[4 * D + 128 * g:4 * D + 128 * g + 128, :])
+        bias = fb[:, 128 * g:128 * g + 128] + jnp.sum(w * vec_ref[3], 0, keepdims=True)
+        w1_ref[:, 128 * g:128 * g + 128] = jnp.concatenate([w * vec_ref[2], two(bias)], 0).astype(bf)
+    w2t_ref[...] = (low_table[...] * 0.5).astype(bf)
+
+    for k in range(line):
+        if k:
+            to_line(k).wait_send()
+        for j in range(plane):
+            if j:
+                to_plane(k, j).wait_send()
+            to_core(k, j).wait_send()
+
+
+def staged(body, hello, ins, outs, *refs):
     a, b = len(ins), len(outs)
     src, dst = refs[:a], refs[a:a + b]
     vin, vout = refs[a + b:2 * a + b], refs[2 * a + b:2 * (a + b)]
     sems, rest = refs[2 * (a + b)], refs[2 * (a + b) + 1:]
+    hello()
     loads = [pltpu.make_async_copy(s, v, sems.at[k]) for k, (s, v) in enumerate(zip(src, vin))]
     for c in loads:
         c.start()
@@ -624,12 +737,12 @@
         c.wait()
 
 
-def staged_call(body, args, shapes, scratch, **params):
+def staged_call(body, args, shapes, scratch, hello=lambda: None, **params):
     hbm = pl.BlockSpec(memory_space=pltpu.HBM)
     ins = [(v.shape, v.dtype) for v in args]
     name = params.pop("name")
     return pl.pallas_call(
-        functools.partial(staged, body, ins, shapes),
+        functools.partial(staged, body, hello, ins, shapes),
         in_specs=[hbm] * len(ins),
         out_specs=[hbm] * len(shapes),
         out_shape=[jax.ShapeDtypeStruct(*s) for s in shapes],
@@ -641,69 +754,49 @@
 
 
 def gather(wire, shards, vectors):
-    shapes = [((FEAT, FF), bf), ((D, 256), bf), ((FEAT, FF), bf), ((D, FF), bf), ((256, 256), bf), ((256, 256), bf),
+    shapes = [((FEAT, FF), bf), ((D, 256), bf), ((FEAT, FF), bf), ((D, FF), bf), ((FF, 256), bf), ((256, 256), bf), ((FF, 256), bf), ((FF, 256), bf),
+              ((256, 256), bf), ((256, 256), bf),
               ((5, D, 128), f32), ((2, 9, 128), f32), ((4, 128), f32)]
     args = [v.T for v in shards] + list(vectors)
     scratch = [
         pltpu.VMEM((wire.n, wire.pad, 128), bf),
-        pltpu.VMEM((wire.pad, 128), bf),
         pltpu.VMEM((wire.pad, D), f32),
         pltpu.VMEM((4 * D + FF, D), f32),
         pltpu.VMEM((D, FF), f32),
+        pltpu.SemaphoreType.DMA((wire.line,)),
         pltpu.SemaphoreType.DMA((wire.chips,)),
         pltpu.SemaphoreType.DMA((wire.chips,)),
         pltpu.SemaphoreType.DMA((wire.n,)),
     ]
     return staged_call(
-        functools.partial(gather_kernel, wire), args, shapes, scratch,
+        functools.partial(gather_kernel, wire), args, shapes, scratch, functools.partial(greet_near, wire),
         vmem_limit_bytes=60 * 2**20, collective_id=0, has_side_effects=True, name="gather_weights")
+
+
+def greet_all(wire):
+    core, q, z = wire.place()
+    me = core * wire.chips + q * wire.line + z
+
+    def one(k, c):
+        pl.semaphore_signal(pltpu.get_barrier_semaphore(), inc=1, device_id=wire.peer(lax.rem(me + k, wire.n)),
+                            device_id_type=MESH)
+        return c
+
+    lax.fori_loop(1, wire.n, one, 0)
 
 
 def reduce_kernel(
     wire, grads, small, res_ref, sum_ref,
-    abuf, comb, bbuf, sbuf, own, gsm, asend, arecv, bsend, brecv, ssend, srecv, gsend, grecv,
+    abuf, sa, comb, scomb, bbuf, sb, comb2, scomb2, cbuf, sc, own, gsm,
+    asend, arecv, sasend, sarecv, bsend, brecv, sbsend, sbrecv, csend, crecv, scsend, screcv, gsend, grecv,
 ):
-    n, nc = wire.n, wire.chips
-    core, chip = wire.place()
+    n, nc, line, plane = wire.n, wire.chips, wire.line, wire.plane
+    core, q, z = wire.place()
     other = 1 - core
-    partner = wire.device(other, chip)
-    me = core * nc + chip
-    barrier = pltpu.get_barrier_semaphore()
+    me = core * nc + q * line + z
 
     def peer(k):
-        slot = lax.rem(me + k, n)
-        return slot, wire.device(slot // nc, lax.rem(slot, nc))
-
-    def greet(k, c):
-        pl.semaphore_signal(barrier, inc=1, device_id=peer(k)[1], device_id_type=MESH)
-        return c
-
-    lax.fori_loop(1, n, greet, 0)
-    pl.semaphore_wait(barrier, n - 1)
-
-    def half(k):
-        to = lax.rem(chip + k, nc)
-        return pltpu.make_async_remote_copy(
-            src_ref=grads.at[other * nc + to], dst_ref=abuf.at[to], send_sem=asend.at[k], recv_sem=arecv.at[to],
-            device_id=partner, device_id_type=MESH)
-
-    def little(k):
-        slot, device = peer(k)
-        return pltpu.make_async_remote_copy(
-            src_ref=small.at[slot], dst_ref=sbuf.at[n - 1 - k], send_sem=ssend.at[k], recv_sem=srecv,
-            device_id=device, device_id_type=MESH)
-
-    def spread(k):
-        slot, device = peer(k)
-        return pltpu.make_async_remote_copy(
-            src_ref=own, dst_ref=gsm.at[n - 1 - k], send_sem=gsend.at[k], recv_sem=grecv,
-            device_id=device, device_id_type=MESH)
-
-    def piece(k):
-        to = lax.rem(chip + k, nc)
-        return pltpu.make_async_remote_copy(
-            src_ref=comb.at[to], dst_ref=bbuf.at[nc - 1 - k], send_sem=bsend.at[k], recv_sem=brecv,
-            device_id=wire.device(core, to), device_id_type=MESH)
+        return wire.peer(lax.rem(me + k, n))
 
     def loop(lo, hi, fn):
         def body(k, c):
@@ -711,34 +804,84 @@
             return c
         lax.fori_loop(lo, hi, body, 0)
 
-    loop(1, n, lambda k: little(k).start())
-    loop(0, nc, lambda k: half(lax.rem(k + 1, nc)).start())
-
-    def merge(k):
-        to = lax.rem(chip + k, nc)
-        half(k).wait_recv()
-        comb[pl.ds(to, 1)] = (grads[pl.ds(core * nc + to, 1)].astype(f32) + abuf[pl.ds(to, 1)].astype(f32)).astype(bf)
-
-    def forward(k):
-        merge(k)
-        piece(k).start()
-
-    loop(1, nc, forward)
-    merge(0)
-
-    pltpu.make_async_copy(sbuf, sbuf, srecv).wait()
-    total = small[pl.ds(me, 1)][0]
-    for k in range(n - 1):
-        total = total + sbuf[k]
+    pl.semaphore_wait(pltpu.get_barrier_semaphore(), n - 1)
+
+    def remote(src, dst, send, recv, device):
+        return pltpu.make_async_remote_copy(
+            src_ref=src, dst_ref=dst, send_sem=send, recv_sem=recv, device_id=device, device_id_type=MESH)
+
+    def plane_at(j):
+        return lax.rem(q + j, plane)
+
+    def line_at(k):
+        return lax.rem(z + k, line)
+
+    partner = wire.device(other, q, z)
+    small_a = remote(small.at[pl.ds(other * nc, nc)], sa, sasend, sarecv, partner)
+
+    def half(j):
+        at = plane_at(j) * line
+        return remote(grads.at[pl.ds(other * nc + at, line)], abuf.at[pl.ds(at, line)], asend.at[j], arecv.at[j], partner)
+
+    def group(j):
+        return remote(comb.at[pl.ds(plane_at(j) * line, line)], bbuf.at[j - 1], bsend.at[j], brecv.at[j],
+                      wire.device(core, plane_at(j), z))
+
+    def small_b(j):
+        return remote(scomb.at[pl.ds(plane_at(j) * line, line)], sb.at[j - 1], sbsend.at[j], sbrecv.at[j],
+                      wire.device(core, plane_at(j), z))
+
+    def last(k):
+        return remote(comb2.at[line_at(k)], cbuf.at[k - 1], csend.at[k], crecv.at[k], wire.device(core, q, line_at(k)))
+
+    def small_c(k):
+        return remote(scomb2.at[line_at(k)], sc.at[k - 1], scsend.at[k], screcv.at[k],
+                      wire.device(core, q, line_at(k)))
+
+    def spread(k):
+        return remote(own, gsm.at[n - 1 - k], gsend.at[k], grecv, peer(k))
+
+    order = list(range(1, plane)) + [0]
+    small_a.start()
+    for j in order:
+        half(j).start()
+    small_a.wait_recv()
+    scomb[...] = small[pl.ds(core * nc, nc)] + sa[...]
+    for j in range(1, plane):
+        small_b(j).start()
+    for j in order:
+        half(j).wait_recv()
+        at = pl.ds(plane_at(j) * line, line)
+        both = grads[pl.ds(core * nc + plane_at(j) * line, line)].astype(f32) + abuf[at].astype(f32)
+        comb[at] = both.astype(bf)
+        if j:
+            group(j).start()
+    mine = pl.ds(q * line, line)
+    total = scomb[mine]
+    for j in range(1, plane):
+        small_b(j).wait_recv()
+        total = total + sb[j - 1]
+    scomb2[...] = total
+    for k in range(1, line):
+        small_c(k).start()
+    total = scomb2[pl.ds(z, 1)][0]
+    for k in range(1, line):
+        small_c(k).wait_recv()
+        total = total + sc[k - 1]
     own[...] = total
     loop(1, n, lambda k: spread(k).start())
-
-    pltpu.make_async_copy(bbuf, bbuf, brecv).wait()
-    total = comb[pl.ds(chip, 1)][0].astype(f32)
-    for k in range(nc - 1):
-        total = total + bbuf[k].astype(f32)
+    total = comb[mine].astype(f32)
+    for j in range(1, plane):
+        group(j).wait_recv()
+        total = total + bbuf[j - 1].astype(f32)
+    comb2[...] = total.astype(bf)
+    for k in range(1, line):
+        last(k).start()
+    total = comb2[pl.ds(z, 1)][0].astype(f32)
+    for k in range(1, line):
+        last(k).wait_recv()
+        total = total + cbuf[k - 1].astype(f32)
     res_ref[...] = total
-
     pltpu.make_async_copy(gsm, gsm, grecv).wait()
     sum_ref[pl.ds(me, 1)] = own[...][None]
 
@@ -746,30 +889,32 @@
         sum_ref[pl.ds(lax.rem(me + n - k, n), 1)] = gsm[pl.ds(n - 1 - k, 1)]
 
     loop(1, n, keep)
-    loop(0, nc, lambda k: half(k).wait_send())
-
-    def done(k):
-        little(k).wait_send()
-        spread(k).wait_send()
-
-    loop(1, n, done)
-    loop(1, nc, lambda k: piece(k).wait_send())
+    small_a.wait_send()
+    for j in range(plane):
+        half(j).wait_send()
+        if j:
+            group(j).wait_send()
+            small_b(j).wait_send()
+    for k in range(1, line):
+        last(k).wait_send()
+        small_c(k).wait_send()
+    loop(1, n, lambda k: spread(k).wait_send())
 
 
 def reduce(wire, grads, small):
-    n, nc = wire.n, wire.chips
+    n, nc, line, plane = wire.n, wire.chips, wire.line, wire.plane
     dma = pltpu.SemaphoreType.DMA
+    big = lambda *lead: pltpu.VMEM(lead + (wire.full, 128), bf)
+    little = lambda *lead: pltpu.VMEM(lead + (8, 128), f32)
     scratch = [
-        pltpu.VMEM((nc, wire.pad, 128), bf),
-        pltpu.VMEM((nc, wire.pad, 128), bf),
-        pltpu.VMEM((nc - 1, wire.pad, 128), bf),
-        pltpu.VMEM((n - 1, 8, 128), f32),
-        pltpu.VMEM((8, 128), f32),
-        pltpu.VMEM((n - 1, 8, 128), f32),
-        dma((nc,)), dma((nc,)), dma((nc,)), dma, dma((n,)), dma, dma((n,)), dma,
+        big(nc), little(nc), big(nc), little(nc), big(plane - 1, line), little(plane - 1, line), big(line),
+        little(line), big(line - 1), little(line - 1), little(), little(n - 1),
+        dma((plane,)), dma((plane,)), dma, dma, dma((plane,)), dma((plane,)), dma((plane,)), dma((plane,)),
+        dma((line,)), dma((line,)), dma((line,)), dma((line,)), dma((n,)), dma,
     ]
     return staged_call(
-        functools.partial(reduce_kernel, wire), (grads, small), [((wire.pad, 128), f32), ((n, 8, 128), f32)], scratch,
+        functools.partial(reduce_kernel, wire), (grads, small), [((wire.full, 128), f32), ((n, 8, 128), f32)], scratch,
+        functools.partial(greet_all, wire),
         vmem_limit_bytes=60 * 2**20, collective_id=1, has_side_effects=True, name="reduce_gradients")
 
 
@@ -779,11 +924,11 @@
 ):
     wide = wire.width
     a, b, c = wire.rows
-    qkv[...] = res[0:a, :wide]
-    proj[...] = res[a:a + b, :wide]
-    fc1[...] = res[a + b:wire.top, :wide]
-    fc2[...] = jnp.concatenate(
-        [res[wire.top + q * wire.low:wire.top + (q + 1) * wire.low, :wide] for q in range(wire.parts)], 1)
+    top, low = wire.unfold(res[...])
+    qkv[...] = top[0:a]
+    proj[...] = top[a:a + b]
+    fc1[...] = top[a + b:wire.top]
+    fc2[...] = jnp.concatenate([low[q * wire.low:(q + 1) * wire.low] for q in range(wire.parts)], 1)
     rel_h[...] = rows[0:REL, :HD]
     rel_w[...] = rows[64:64 + REL, :HD]
     for k in range(9):
@@ -815,9 +960,9 @@
     canvases = block_input.shape[0]
     whole = lambda v: pl.BlockSpec(v.shape, lambda i, n=v.ndim: (0,) * n)
     per = lambda: pl.BlockSpec((PAIR, D, NTOK), lambda i: (i, 0, 0))
-    packed = [((wire.n, wire.pad, 128), bf), ((wire.n * 8, 128), f32)]
+    packed = [((wire.n, wire.full, 128), bf), ((wire.n * 8, 128), f32)]
     results = pl.pallas_call(
-        functools.partial(kernel, wire),
+        functools.partial(kernel, wire, canvases // PAIR),
         grid=(canvases // PAIR,),
         in_specs=[pl.BlockSpec(memory_space=pltpu.SMEM), per(), per()] + [whole(v) for v in consts],
         out_specs=[per(), per()] + [pl.BlockSpec(s, lambda i, n=len(s): (0,) * n) for s, _ in packed],
@@ -826,7 +971,7 @@
         scratch_shapes=[
             pltpu.VMEM((FEAT, FF), f32), pltpu.VMEM((D, 256), f32), pltpu.VMEM((FEAT, FF), f32),
             pltpu.VMEM((D, FF), f32), pltpu.VMEM((256, 256), f32), pltpu.VMEM((9, 4, 8, 128), f32),
-            pltpu.VMEM((2, 4, 8, 128), f32), pltpu.VMEM((5, D, 128), f32), pltpu.VMEM((5, D, 16), f32),
+            pltpu.VMEM((2, 4, 8, 128), f32), pltpu.VMEM((D, 128), f32), pltpu.VMEM((D, 16), f32),
             pltpu.VMEM((4 * D + FF, D), f32), pltpu.VMEM((wire.pad, D), f32),
             pltpu.VMEM((PAIR, 4, KVROWS, 128), f32),
             pltpu.VMEM((PAIR, 4, 272, 128), f32),
@@ -834,6 +979,9 @@
             pltpu.VMEM((PAIR, 2, 256, 256), bf),
             pltpu.VMEM((PAIR, 2, 256, 256), bf),
             pltpu.VMEM((PAIR, 2, 256, 256), bf),
+        ] + [
+            pltpu.VMEM(v, bf) for rows, cols in ((FEAT, FF), (D, 256), (FEAT, FF), (D, FF))
+            for v in ((canvases // PAIR, rows, PAIR * REST), (canvases * REST, cols))
         ],
         compiler_params=pltpu.CompilerParams(vmem_limit_bytes=60 * 2**20),
         name="block_step",

time: 186 us -> 169 us (0.909)
  Pallas kernels: 186 us -> 168 us
    pallas_call x4, Pallas kernels: 186 us -> 168 us  [the longest x1 125 us: compute(): pl.pallas_call(functools.partial(kernel, wire, canvases // PAIR), grid=(c...]
where the time goes in v3:
time: 169 us
  Pallas kernels  168 us (99%)
    pallas_call x1, Pallas kernels, compute(): pl.pallas_call(functools.partial(kernel, wire, canvases // PAIR), grid=(c...  125 us
    pallas_call x3, Pallas kernels, staged_call(): pl.pallas_call(functools.partial(staged, body, hello, ins, shapes), in_sp...  43.5 us

profile of v3, /device:TPU:0, one launch (start us, length us, event | category | flops | bytes accessed | tf_op | source)
XLA Modules:
  0.0 169.2 jit_solution(5668216186458521063)
XLA Ops:
  0.7 19.4 %gather_weights.1 = (bf16[208,768]{1,0:T(8,128)(2,1)}, bf16[192,256]{1,0:T(8,128)(2,1)}, bf16[208,768]{1,0:T(8,128)(2,1)}, bf16[192,768]{1,0:T(8,128)(2,1)}, bf1...) custom-call(bf16[36,96]{1,0:T(8,128)(2,1)} %bitcast.22, ...), custom_call_target="tpu_custom_call" | custom-call | tf_op jit(solution)/shard_map/gather_weights/pallas_call | solution.py:744
  20.1 124.8 %block_step.1 = (bf16[16,192,784]{2,1,0:T(8,128)(2,1)}, f32[16,192,784]{2,1,0:T(8,128)}, bf16[32,112,128]{2,1,0:T(8,128)(2,1)}, f32[256,128]{1,0:T(8,128)}) custom-call(s32[16,196]{1,0:T(8,128)} %kc_ref.1, bf16[16,192,784]{2,1,0:T(8,128)(2,1)} %bitcast.16, bf16[16,192,784]{2,1,0:T(8,128)(2,1)} %bitcast.17, bf16[208,768]{1,0:T(8,128)(2,1)} %get-tuple-element.55.wq_ref, ...), custom_call_target="tpu_custom_call" | custom-call | tf_op jit(solution)/shard_map/block_step/pallas_call | solution.py:964
  145.0 22.1 %reduce_gradients.1 = (f32[112,128]{1,0:T(8,128)}, f32[32,8,128]{2,1,0:T(8,128)}) custom-call(bf16[32,112,128]{2,1,0:T(8,128)(2,1)} %get-tuple-element.70.refs_0_, f32[32,8,128]{2,1,0:T(8,128)} %bitcast.19), custom_call_target="tpu_custom_call" | custom-call | tf_op jit(solution)/shard_map/reduce_gradients/pallas_call | solution.py:744
  167.1 2.0 %split_gradients.1 = (f32[36,96]{1,0:T(8,128)}, f32[12,96]{1,0:T(8,128)}, f32[48,96]{1,0:T(8,128)}, f32[12,384]{1,0:T(8,128)}, f32[576]{0:T(1024)}, /*index=5*/f...) custom-call(f32[112,128]{1,0:T(8,128)} %get-tuple-element.72.refs_0_, ...), custom_call_target="tpu_custom_call" | custom-call | tf_op jit(solution)/shard_map/split_gradients/pallas_call | solution.py:744

commit v4 on v3

--- a/solution.py
+++ b/solution.py
@@ -20,14 +20,13 @@
 EPS = 1e-06
 FILL = -1e30
 LOG2E = 1.4426950408889634
-LN2 = 0.6931471805599453
 SCALE = HD ** (-0.5)
 BASE = 32
 KVROWS = BASE + NTOK + 24
 bf = jnp.bfloat16
 PAIR = 2
-SKEW = 8
-EVERY = 1
+SKEW = 9
+EVERY = 9
 FEAT = 208
 MAIN = 768
 REST = 16
@@ -153,8 +152,10 @@
     def _():
         for ref in (gq_ref, gp_ref, g1_ref, g2_ref, grel_ref, gpk_ref, gpv_ref, gln_ref, tail_ref):
             ref[...] = jnp.zeros_like(ref)
-        kvs[...] = jnp.zeros_like(kvs)
-        gps[...] = jnp.zeros_like(gps)
+        for c, n in [(c, n) for c in range(PAIR) for n in range(4)]:
+            kvs[c, n, 0:BASE, :] = jnp.zeros((BASE, 128), f32)
+            kvs[c, n, BASE + NTOK:KVROWS, :] = jnp.zeros((KVROWS - BASE - NTOK, 128), f32)
+            gps[c, n, 224:272, :] = jnp.zeros((48, 128), f32)
         key = iota((256, 128), 0)
         lane = iota((256, 128), 1)
         ki = key >> 4
@@ -237,7 +238,7 @@
             part = piece[:, f * wide:(f + 1) * wide]
             wire_ref[wire.slot(d, f)] = wire.fold(part[:wire.top], part[wire.top:wire.used]).astype(bf)
     small_ref[...] = jnp.zeros_like(small_ref)
-    turned = jnp.transpose(grel_ref[...]) * LOG2E
+    turned = jnp.transpose(grel_ref[...])
     small_ref[0:64] = turned[0:64, 0:128] + turned[64:128, 128:256]
     small_ref[64:128] = turned[192:256, 0:128] + turned[128:192, 128:256]
     for w in range(2):
@@ -309,9 +310,12 @@
     x = x_ref[slot].astype(f32)
     u1, r1 = norm_cols(x)
     nb = with_ones(u1.astype(bf))
-    qb = dot_tn(nb, wq_ref[:, :256]).astype(bf)
-    for n in range(4):
-        kvs[n, BASE:BASE + NTOK, :] = dot_tn(nb, wq_ref[:, 256 + 128 * n:384 + 128 * n])
+    nt = jnp.transpose(nb)
+    qb = dot(nt, wq_ref[:, :256]).astype(bf)
+    for w in range(2):
+        both = dot(nt, wq_ref[:, 256 + 256 * w:512 + 256 * w])
+        kvs[2 * w, BASE:BASE + NTOK, :] = both[:, :128]
+        kvs[2 * w + 1, BASE:BASE + NTOK, :] = both[:, 128:]
 
     yield
     notfirst = (iota((16, 128), 0) > 0).astype(f32)
@@ -340,8 +344,8 @@
         yield
         h = n % 2
         if w == 0:
+            kb[h, 0:224, :128] = (val * SCALE).astype(bf)
             val = val * (SCALE * LOG2E)
-            kb[h, 0:224, :128] = val.astype(bf)
             pad = ((iota((224, 128), 0) & 15) >= KS) & (iota((224, 128), 1) == HD)
             kf[h, 0:224, :128] = jnp.where(pad, FILL, val).astype(bf)
         else:
@@ -362,8 +366,8 @@
     col_bias = jnp.where((y56 >= col_cut) != col_side, FILL, 0.0)
 
     yield
-    a_h = dot(qb, relf_ref[:, :128])
-    a_w = dot(qb, relf_ref[:, 128:])
+    a_both = dot(qb, relf_ref[...])
+    a_h, a_w = a_both[:, :128], a_both[:, 128:]
     pieces_h = roll_x(a_h)
     yield
     pieces_w = roll_y(a_w)
@@ -387,28 +391,30 @@
         o = dot(e, vx[h])
         rinv = 1.0 / o[:, 128:]
         eb.append(e)
-        inv.append(rinv * LN2)
+        inv.append(rinv)
         mixed.append(o[:, :128] * rinv)
     yield
     ab = (jnp.concatenate(mixed, 1) + qb.astype(f32)).astype(bf)
 
     yield
-    middle = x + features(ab, wp_ref[...])
+    middle = x + dot_nt(wpt_ref[...], ab)
     u2, r2 = norm_cols(middle)
     n2b = with_ones(u2.astype(bf))
     gb = g_ref[slot]
+    n2t, gt = jnp.transpose(n2b), jnp.transpose(gb)
     yield
     act, gh = [], []
     for n in range(3):
         cols = slice(256 * n, 256 * n + 256)
-        hid = dot_tn(n2b, w1_ref[:, cols])
-        gact = dot_tn(gb, w2t_ref[:, cols])
+        hid = dot(n2t, w1_ref[:, cols])
+        gact = dot(gt, w2t_ref[:, cols])
         yield
-        z = hid * 0.7071067811865476
-        phi = 1.0 + lax.erf(z)
-        slope = phi + z * (jnp.exp2(z * z * (-LOG2E)) * 1.1283791670955126)
-        act.append((hid * phi).astype(bf))
-        gh.append((gact * slope).astype(bf))
+        hid = hid.astype(bf)
+        z = hid * bf(0.7071067811865476)
+        phi = bf(1.0) + lax.erf(z)
+        slope = phi + z * (jnp.exp2(z * z * bf(-LOG2E)) * bf(1.1283791670955126))
+        act.append(hid * phi)
+        gh.append(gact.astype(bf) * slope)
         yield
     act = jnp.concatenate(act, 1)
     gh = jnp.concatenate(gh, 1)
@@ -454,11 +460,12 @@
     for n in range(4):
         w, h = n // 2, n % 2
         if w == 0:
-            qt = dot_tn(qb[:, 128 * h:128 * h + 128], jnp.concatenate([dss[h], gab], 1))
-            grel_ref[128 * h:128 * h + 128] += qt[:, 256:]
-            e = jnp.transpose(qt[:, :256])[:224] * (SCALE * LOG2E)
+            qt = dot_tn(qb[:, 128 * h:128 * h + HD], jnp.concatenate([dss[h], gab], 1))
+            grel_ref[128 * h:128 * h + HD] += qt[:, 256:]
+            e = jnp.transpose(qt[:, :256])[:224] * SCALE
         else:
-            e = jnp.transpose(dot_tn(g2bs[h], eb[h]))[:224] * LOG2E
+            e = jnp.transpose(dot_tn(g2bs[h][:, :HD], eb[h]))[:224]
+        e = jnp.concatenate([e, jnp.zeros((224, 128 - HD), f32)], 1)
         yield
         gpv_ref[0, n] += fold(e * u_pool[n])
         gpv_ref[1, n] += fold(e)
@@ -522,6 +529,9 @@
         self.parts = FF // fsdp // self.width
         self.used = self.top + self.parts * self.low
         self.pad = -(-self.used // 16) * 16
+        self.tile = 128 if FF // fsdp % 128 == 0 else FF // fsdp
+        self.tiles = FF // fsdp // self.tile
+        self.load = -(-(self.top + self.tiles * self.low) // 16) * 16
         self.lows = self.parts * self.low
         self.dense = self.width == 96 and self.top == 2 * self.lows and self.lows % 48 == 0
         self.full = self.top + self.lows // 3 if self.dense else self.pad
@@ -596,10 +606,10 @@
     tmp[a:a + b, :wide] = proj[...].astype(f32)
     tmp[a + b:wire.top, :wide] = fc1[...].astype(f32)
     below = fc2[...].astype(f32)
-    for p in range(wire.parts):
+    for p in range(wire.tiles):
         first = wire.top + p * wire.low
-        tmp[first:first + wire.low, :wide] = below[:, p * wide:(p + 1) * wide]
-    buf[pl.ds(me, 1)] = tmp[:, :128].astype(bf)[None]
+        tmp[first:first + wire.low, :wire.tile] = below[:, p * wire.tile:(p + 1) * wire.tile]
+    buf[pl.ds(me, 1)] = tmp[...].astype(bf)[None]
     pl.semaphore_wait(pltpu.get_barrier_semaphore(), line + plane - 1)
 
     def held(k, j):
@@ -633,7 +643,7 @@
     zero32 = jnp.zeros((64, 128 - HD), f32)
 
     def tall(ref):
-        t = jnp.concatenate([ref[...] * LOG2E, jnp.zeros((64 - REL, HD), f32)], 0)
+        t = jnp.concatenate([ref[...], jnp.zeros((64 - REL, HD), f32)], 0)
         t = jnp.concatenate([t, zero32], 1)
         return jnp.where(iota((64, 128), 0) < 54, t, 0.0)
 
@@ -641,11 +651,11 @@
     none = jnp.zeros((64, 128), f32)
     relb = jnp.concatenate([
         jnp.concatenate([th, none], 1), jnp.concatenate([none, th], 1),
-        jnp.concatenate([none, tw], 1), jnp.concatenate([tw, none], 1)], 0).astype(bf)
-    relb_ref[...] = relb
+        jnp.concatenate([none, tw], 1), jnp.concatenate([tw, none], 1)], 0)
+    relb_ref[...] = relb.astype(bf)
     at, to = iota((256, 256), 0), iota((256, 256), 1)
     mirror = ((at >> 6) == (to >> 6)) & ((at & 63) + (to & 63) == 53)
-    relf_ref[...] = dot_tn(relb, jnp.where(mirror, 1.0, 0.0).astype(bf)).astype(bf)
+    relf_ref[...] = dot_tn((relb * LOG2E).astype(bf), jnp.where(mirror, 1.0, 0.0).astype(bf)).astype(bf)
     for w in range(2):
         taps = jnp.concatenate([pool_kernel[k, w:w + 1, :] for k in range(9)], 0)
         pk_ref[w] = jnp.concatenate([taps, jnp.zeros((9, 128 - HD), f32)], 1)
@@ -666,14 +676,13 @@
 
     for d in range(wire.dp):
         blocks = [buf[wire.slot(d, f)].astype(f32) for f in range(wire.fsdp)]
-        tmp[...] = jnp.concatenate([v[:, :wide] for v in blocks], 1)
+        top = jnp.concatenate([v[:wire.top, :wide] for v in blocks], 1)
         for first, count, to_row in wire.starts(d):
-            table[to_row:to_row + count, :] = tmp[first:first + count, :]
-        for f in range(wire.fsdp):
-            parts = [tmp[wire.top + q * wire.low:wire.top + (q + 1) * wire.low, f * wide:(f + 1) * wide]
-                     for q in range(wire.parts)]
-            low_table[wire.low * d:wire.low * (d + 1), f * wide * wire.parts:(f + 1) * wide * wire.parts] = (
-                jnp.concatenate(parts, 1))
+            table[to_row:to_row + count, :] = top[first:first + count, :]
+        for f, v in enumerate(blocks):
+            for p in range(wire.tiles):
+                first, at = wire.top + p * wire.low, (f * wire.tiles + p) * wire.tile
+                low_table[wire.low * d:wire.low * (d + 1), at:at + wire.tile] = v[first:first + wire.low, :wire.tile]
 
     def two(bias):
         hi = bias.astype(bf).astype(f32)
@@ -759,8 +768,8 @@
               ((5, D, 128), f32), ((2, 9, 128), f32), ((4, 128), f32)]
     args = [v.T for v in shards] + list(vectors)
     scratch = [
-        pltpu.VMEM((wire.n, wire.pad, 128), bf),
-        pltpu.VMEM((wire.pad, D), f32),
+        pltpu.VMEM((wire.n, wire.load, 128), bf),
+        pltpu.VMEM((wire.load, 128), f32),
         pltpu.VMEM((4 * D + FF, D), f32),
         pltpu.VMEM((D, FF), f32),
         pltpu.SemaphoreType.DMA((wire.line,)),

time: 169 us -> 152 us (0.90)
  Pallas kernels: 168 us -> 151 us
    pallas_call x1, Pallas kernels: 125 us -> 109 us  [compute(): pl.pallas_call(functools.partial(kernel, wire, canvases // PAIR), grid=(c...]
where the time goes in v4:
time: 152 us
  Pallas kernels  151 us (99%)
    pallas_call x1, Pallas kernels, compute(): pl.pallas_call(functools.partial(kernel, wire, canvases // PAIR), grid=(c...  109 us
    pallas_call x3, Pallas kernels, staged_call(): pl.pallas_call(functools.partial(staged, body, hello, ins, shapes), in_sp...  42.2 us

profile of v4, /device:TPU:0, one launch (start us, length us, event | category | flops | bytes accessed | tf_op | source)
XLA Modules:
  0.0 152.1 jit_solution(1339366689510606112)
XLA Ops:
  0.7 18.2 %gather_weights.1 = (bf16[208,768]{1,0:T(8,128)(2,1)}, bf16[192,256]{1,0:T(8,128)(2,1)}, bf16[208,768]{1,0:T(8,128)(2,1)}, bf16[192,768]{1,0:T(8,128)(2,1)}, bf1...) custom-call(bf16[36,96]{1,0:T(8,128)(2,1)} %bitcast.22, ...), custom_call_target="tpu_custom_call" | custom-call | tf_op jit(solution)/shard_map/gather_weights/pallas_call | solution.py:753
  18.8 109.2 %block_step.1 = (bf16[16,192,784]{2,1,0:T(8,128)(2,1)}, f32[16,192,784]{2,1,0:T(8,128)}, bf16[32,112,128]{2,1,0:T(8,128)(2,1)}, f32[256,128]{1,0:T(8,128)}) custom-call(s32[16,196]{1,0:T(8,128)} %kc_ref.1, bf16[16,192,784]{2,1,0:T(8,128)(2,1)} %bitcast.16, bf16[16,192,784]{2,1,0:T(8,128)(2,1)} %bitcast.17, bf16[208,768]{1,0:T(8,128)(2,1)} %get-tuple-element.55.wq_ref, ...), custom_call_target="tpu_custom_call" | custom-call | tf_op jit(solution)/shard_map/block_step/pallas_call | solution.py:973
  128.1 22.1 %reduce_gradients.1 = (f32[112,128]{1,0:T(8,128)}, f32[32,8,128]{2,1,0:T(8,128)}) custom-call(bf16[32,112,128]{2,1,0:T(8,128)(2,1)} %get-tuple-element.70.refs_0_, f32[32,8,128]{2,1,0:T(8,128)} %bitcast.19), custom_call_target="tpu_custom_call" | custom-call | tf_op jit(solution)/shard_map/reduce_gradients/pallas_call | solution.py:753
  150.2 2.0 %split_gradients.1 = (f32[36,96]{1,0:T(8,128)}, f32[12,96]{1,0:T(8,128)}, f32[48,96]{1,0:T(8,128)}, f32[12,384]{1,0:T(8,128)}, f32[576]{0:T(1024)}, /*index=5*/f...) custom-call(f32[112,128]{1,0:T(8,128)} %get-tuple-element.72.refs_0_, ...), custom_call_target="tpu_custom_call" | custom-call | tf_op jit(solution)/shard_map/split_gradients/pallas_call | solution.py:753
